TPU v7x, 512 devices: a whole 4x8x8 slice. The times are simulated.
512 devices in a mesh: dp: 8 (over y_hi, core), width: 8 (over z), hidden: 8 (over y_lo, x).
Axes of the slice: x: 4, y: 8 (y_hi: 4, y_lo: 2; y = y_hi * 2 + y_lo), z: 8, core: 2. Of those that a mesh axis runs over, the one named last changes fastest.
Arguments:
- tokens: bfloat16 [1024, 4096], P('dp', 'width'), may hold values from -6 to 6
- token_job_index: int32 [1024], P('dp'), may hold values from 0 to 15, as said below
- gate_up_matrix: bfloat16 [2, 4096, 14336], P(None, 'width', ('dp', 'hidden')), may hold values from -0.09375 to 0.09375
- down_matrix: bfloat16 [14336, 4096], P(('dp', 'hidden'), 'width'), may hold values from -0.125 to 0.125
- adapter_input_maps: bfloat16 [2, 4096, 256], P(None, 'width'), may hold values from -0.09375 to 0.09375
- adapter_output_maps: bfloat16 [2, 256, 14336], P(None, None, ('dp', 'hidden')), may hold values from -1.5 to 1.5
- cotangent: bfloat16 [1024, 4096], P('dp', ('width', 'hidden')), may hold values from -6 to 6
Outputs:
- mixed: bfloat16 [1024, 4096], P('dp', ('width', 'hidden'))
- input_gradient: bfloat16 [1024, 4096], P('dp', ('width', 'hidden'))
- adapter_input_gradient: float32 [2, 4096, 256], P(None, 'width')
- adapter_output_gradient: float32 [2, 256, 14336], P(None, None, ('dp', 'hidden'))
Inputs may be any that keep to these rules, and one draw needn't show every extreme that they name: `token_job_index`: constant on aligned blocks of 128 tokens; 0 and 15 occur in every draw.
All inputs are finite; a program needn't handle non-finite values.
Results may differ from a plain program's by a relative error of at most 0.014.
Values may be sent and summed in bfloat16 or wider, within the bound.
A program may use at most 64 MiB of HBM per device.

v0:
```python
import jax
import jax.numpy as jnp
from jax import lax
from jax.sharding import PartitionSpec as P

JOB_COUNT = 16
ADAPTER_RANK = 16
JOB_ROWS = 128


adapter_scale = 0.5


def settle_stationary(partial_sums, dp_count, hid_count):
    all_rows, width_cols = partial_sums.shape
    block_sums = partial_sums.reshape(
        dp_count, all_rows // dp_count, hid_count, width_cols // hid_count
    )
    block_sums = block_sums.transpose(0, 2, 1, 3).reshape(
        dp_count * hid_count, all_rows // dp_count, width_cols // hid_count
    )
    return lax.psum_scatter(block_sums, ("dp", "hidden"), scatter_dimension=0, tiled=True)[0]


def select_columns(block_lookup, adapter_in):
    pairs, feat_cols, all_cols = adapter_in.shape
    grouped = adapter_in.reshape(pairs, feat_cols, JOB_COUNT, all_cols // JOB_COUNT)
    return jnp.einsum(
        "bj,kdjr->kbdr", block_lookup, grouped, preferred_element_type=jnp.float32
    ).astype(jnp.bfloat16)


def pick_rows(block_lookup, adapter_out):
    pairs, all_rows, hid_cols = adapter_out.shape
    grouped = adapter_out.reshape(pairs, JOB_COUNT, all_rows // JOB_COUNT, hid_cols)
    return jnp.einsum(
        "bj,kjrf->kbrf", block_lookup, grouped, preferred_element_type=jnp.float32
    ).astype(jnp.bfloat16)


def local(
    tokens,
    token_job_index,
    gate_up_matrix,
    down_matrix,
    adapter_input_maps,
    adapter_output_maps,
    cotangent,
):
    dp_count = lax.axis_size("dp")
    hid_count = lax.axis_size("hidden")
    own_rows, feat_cols = tokens.shape
    own_blocks = own_rows // JOB_ROWS
    block_job = token_job_index.reshape(own_blocks, JOB_ROWS)[:, 0]
    job_range = jnp.arange(JOB_COUNT, dtype=jnp.int32)
    job_lookup = (block_job[:, None] == job_range[None, :]).astype(jnp.bfloat16)
    job_columns = select_columns(job_lookup, adapter_input_maps)
    token_row_blocks = tokens.reshape(own_blocks, JOB_ROWS, feat_cols)
    low_part = jnp.einsum(
        "hfi,uhiy->uhfy", token_row_blocks, job_columns, preferred_element_type=jnp.float32
    )
    low_part = lax.psum(low_part, "width")
    reduced_inner = low_part.astype(jnp.bfloat16)
    gate_up_result, output_map_slice, down_result = (
        gate_up_matrix,
        adapter_output_maps,
        down_matrix,
    )
    row_blocks, inner_rows, block_lookup = (
        lax.all_gather(token_row_blocks, "dp", axis=0, tiled=True),
        lax.all_gather(reduced_inner, "dp", axis=1, tiled=True),
        lax.all_gather(job_lookup, "dp", axis=0, tiled=True),
    )
    block_count = row_blocks.shape[0]
    row_total = block_count * JOB_ROWS
    hid_cols = gate_up_result.shape[2]
    rank_columns = select_columns(block_lookup, adapter_input_maps)
    rank_rows = pick_rows(block_lookup, output_map_slice)
    row_flat = row_blocks.reshape(row_total, feat_cols)
    frozen_sums = jnp.einsum(
        "rd,kdf->krf", row_flat, gate_up_result, preferred_element_type=jnp.float32
    )
    frozen_sums = lax.psum(frozen_sums, "width")
    adapter_contribution = jnp.einsum(
        "kbqr,kbrf->kbqf", inner_rows, rank_rows, preferred_element_type=jnp.float32
    ).reshape(2, row_total, hid_cols)
    before_activation = frozen_sums + adapter_scale * adapter_contribution
    gate_pre = before_activation[0]
    up_pre = before_activation[1]
    sigmoid_gate = jax.nn.sigmoid(gate_pre)
    silu_gate = gate_pre * sigmoid_gate
    hidden_state = (silu_gate * up_pre).astype(jnp.bfloat16)
    partial_out = jnp.dot(hidden_state, down_result, preferred_element_type=jnp.float32)
    mixed = settle_stationary(partial_out, dp_count, hid_count).astype(jnp.bfloat16)
    gathered = lax.all_gather(cotangent[None], ("dp", "hidden"), axis=0, tiled=True)
    tok_rows = gathered.shape[1]
    piece_cols = gathered.shape[2]
    cot_rows = (
        gathered.reshape(dp_count, hid_count, tok_rows, piece_cols)
        .transpose(0, 2, 1, 3)
        .reshape(dp_count * tok_rows, hid_count * piece_cols)
    )
    hidden_grad = jnp.einsum("rd,fd->rf", cot_rows, down_result, preferred_element_type=jnp.float32)
    hidden_grad = lax.psum(hidden_grad, "width")
    gate_grad = hidden_grad * up_pre * sigmoid_gate * (1.0 + gate_pre * (1.0 - sigmoid_gate))
    up_grad = hidden_grad * silu_gate
    before_activation_gradient = jnp.stack([gate_grad, up_grad]).astype(jnp.bfloat16)
    grad_blocks = before_activation_gradient.reshape(2, block_count, JOB_ROWS, hid_cols)
    backward_inner = adapter_scale * jnp.einsum(
        "kbqf,kbrf->kbqr", grad_blocks, rank_rows, preferred_element_type=jnp.float32
    )
    grad_part = jnp.einsum(
        "krf,kdf->rd",
        before_activation_gradient,
        gate_up_result,
        preferred_element_type=jnp.float32,
    )
    adapter_back = jnp.einsum(
        "japx,jatx->apt",
        backward_inner,
        rank_columns.astype(jnp.float32),
        precision=lax.Precision.HIGHEST,
    )
    grad_part = grad_part + adapter_back.reshape(row_total, feat_cols)
    input_gradient = settle_stationary(grad_part, dp_count, hid_count).astype(jnp.bfloat16)
    table_wide = block_lookup.astype(jnp.float32)
    a_blocks = jnp.einsum(
        "aph,mapc->mahc",
        row_blocks.astype(jnp.float32),
        backward_inner,
        precision=lax.Precision.HIGHEST,
    )
    input_map_piece = jnp.einsum(
        "kbdr,bj->kdjr", a_blocks, table_wide, precision=lax.Precision.HIGHEST
    ).reshape(2, feat_cols, JOB_COUNT * ADAPTER_RANK)
    adapter_input_gradient = lax.psum(input_map_piece, ("dp", "hidden"))
    output_map_blocks = adapter_scale * jnp.einsum(
        "kbqr,kbqf->kbrf", inner_rows, grad_blocks, preferred_element_type=jnp.float32
    )
    output_map_piece = jnp.einsum(
        "kbrf,bj->kjrf", output_map_blocks, table_wide, precision=lax.Precision.HIGHEST
    ).reshape(2, JOB_COUNT * ADAPTER_RANK, hid_cols)
    return (mixed, input_gradient, adapter_input_gradient, output_map_piece)


def solution(mesh):
    return jax.shard_map(
        local,
        mesh=mesh,
        in_specs=(
            P("dp", "width"),
            P("dp"),
            P(None, "width", ("dp", "hidden")),
            P(("dp", "hidden"), "width"),
            P(None, "width", None),
            P(None, None, ("dp", "hidden")),
            P("dp", ("width", "hidden")),
        ),
        out_specs=(
            P("dp", ("width", "hidden")),
            P("dp", ("width", "hidden")),
            P(None, "width", None),
            P(None, None, ("dp", "hidden")),
        ),
        check_vma=False,
    )
```

profile of v0, /device:TPU:64, one launch (start us, length us, event | category | flops | bytes accessed | tf_op | source)
XLA Modules:
  0.0 1027.9 jit_solution(10063531487244204358)
XLA Ops:
  7.2 0.7 all-gather.6.cloned.1.call-update
  8.0 0.7 all-gather.8.cloned.1.call-update
  8.7 37.3 %all-gather.6.cloned.1.call-done = bf16[1024,512]{1,0:T(8,128)(2,1)} async-done(((bf16[128,512]{1,0:T(8,128)(2,1)}), bf16[1024,512]{1,0:T(8,128)(2,1)}) %all-gather.6.cloned.1.call-update) | async-done | bytes 1048592 | tf_op jit(solution)/shard_map/all_gather | solution.py:70
  46.1 3.2 convolution_bitcast_fusion
  49.2 145.3 %all-gather.8.cloned.1.call-done = bf16[8192,64]{0,1:T(8,128)(2,1)} async-done(((bf16[128,64]{0,1:T(8,128)(2,1)}), bf16[8192,64]{0,1:T(8,128)(2,1)}) %all-gather.8.cloned.1.call-update) | async-done | bytes 1048592 | tf_op jit(solution)/shard_map/all_gather | solution.py:95
  194.5 1.5 copy.98
  196.0 0.1 copy.72
  196.2 1.3 fusion.2
  197.6 0.9 copy.70
  198.5 0.1 copy.65
  198.7 11.8 %all-gather.2 = bf16[8,1,16]{2,1,0:T(2,128)(2,1)S(1)} all-gather(bf16[1,1,16]{2,1,0:T(2,128)(2,1)S(1)} %fusion.42), channel_id=1, replica_groups=mesh['dp'=8,'width'=8,'hidden'=8] {'dp'}, dimensions={0}, use_global_device_ids=true | all-gather | bytes 288 | tf_op jit(solution)/shard_map/all_gather | solution.py:72
  210.5 0.2 copy.64
  210.7 0.4 fusion.19
  211.2 0.1 convolution_bitcast_fusion.4
  211.3 28.9 %psum.29 = bf16[2,1,128,16]{2,3,0,1:T(8,128)(2,1)S(1)} all-reduce(f32[2,1,128,16]{2,3,0,1:T(8,128)S(1)} %convolution_bitcast_fusion.4), channel_id=1, replica_groups=mesh['dp'=8,'width'=8,'hidden'=8] {'width'}, use_global_device_ids=true, to_apply=%region_1.0 | all-reduce | flops 4096 | bytes 24576 | tf_op jit(solution)/shard_map/psum | solution.py:62
  240.2 14.8 %all_gather.13 = bf16[2,8,128,16]{2,3,0,1:T(8,128)(2,1)S(1)} all-gather(bf16[2,1,128,16]{2,3,0,1:T(8,128)(2,1)S(1)} %psum.29), channel_id=1, replica_groups=mesh['dp'=8,'width'=8,'hidden'=8] {'dp'}, dimensions={1}, use_global_device_ids=true | all-gather | bytes 73728 | tf_op jit(solution)/shard_map/all_gather | solution.py:71
  255.0 0.2 fusion.1
  255.2 1.7 multiply_bitcast_fusion
  257.0 33.3 %all-reduce.6.cloned.1.call-done = (f32[2,1024,224]{1,2,0:T(8,128)}, f32[1024,224]{0,1:T(8,128)}) async-done(((f32[2,1024,224]{1,2,0:T(8,128)}, f32[1024,224]{0,1:T(8,128)}), (f32[2,1024,224]{1,2,0:T(8,128)}, f32[1024,224]{0,1:T(8,128)})) %all-reduce.6.cloned.1.call-update) | async-done | bytes 2752528 | tf_op jit(solution)/shard_map/psum | solution.py:83
  290.3 2.4 bitcast_add_fusion.1
  292.6 0.6 fusion.16
  293.6 0.4 copy-done.4
  294.0 0.2 copy-done.6
  294.1 0.3 convolution_multiply_fusion.1
  294.5 0.3 copy-done.3
  294.8 0.5 convolution_bitcast_fusion.3
  295.3 0.8 convolution_bitcast_fusion.1
  296.1 1.6 copy.82
  297.8 0.2 fusion.24
  298.1 0.6 copy-done.8
  298.7 1.8 fusion.22
  300.5 0.2 reduce-scatter.5.cloned.1.call-start
  300.8 0.4 fusion
  301.2 1.0 fusion.26
  302.2 0.7 bitcast_add_fusion
  303.0 1.8 copy.78
  304.8 2.1 copy.102
  306.9 1.7 copy.79
  308.6 0.6 convolution_multiply_fusion
  309.2 0.5 convolution_bitcast_fusion.2
  309.7 0.3 copy.85
  310.0 1.0 copy.87
  310.9 181.6 %all-reduce.4.cloned.1.call-done = f32[2,512,256]{1,2,0:T(8,128)} async-done(((f32[2,512,256]{1,2,0:T(8,128)}), f32[2,512,256]{1,2,0:T(8,128)}) %all-reduce.4.cloned.1.call-update) | async-done | bytes 1048592 | tf_op jit(solution)/shard_map/psum | solution.py:136
  492.5 2.5 copy.86
  495.1 261.6 %reduce-scatter.3.cloned.1.call-done = f32[1,128,64]{1,2,0:T(8,128)} async-done(((f32[64,128,64]{1,2,0:T(8,128)}), f32[1,128,64]{1,2,0:T(8,128)}) %reduce-scatter.3.cloned.1.call-update) | async-done | bytes 32784 | tf_op jit(solution)/shard_map/reduce_scatter | solution.py:22
  756.7 1.4 convert_bitcast_fusion.1
  758.0 261.6 %reduce-scatter.5.cloned.1.call-done = f32[1,128,64]{1,2,0:T(8,128)} async-done(((f32[64,128,64]{1,2,0:T(8,128)}), f32[1,128,64]{1,2,0:T(8,128)}) %reduce-scatter.5.cloned.1.call-update) | async-done | bytes 32784 | tf_op jit(solution)/shard_map/reduce_scatter | solution.py:22
  1019.6 1.4 convert_bitcast_fusion
  (42 shorter events, 0.8 us)
Async XLA Ops:
  7.2 38.9 %copy-start = (bf16[2,512,224]{1,2,0:T(8,128)(2,1)S(1)}, bf16[2,512,224]{1,2,0:T(8,128)(2,1)}, u32[]{:S(2)}) copy-start(bf16[2,512,224]{1,2,0:T(8,128)(2,1)} %param.9) | copy-start | bytes 1376260
  7.2 38.9 %all-gather.6.cloned.1.call-start = ((), (), s32[]{:S(2)}) async-start(), calls=%async_computation.5 | async-start | bytes 1179648 | tf_op jit(solution)/shard_map/all_gather | solution.py:70
  7.9 186.6 %all-gather.8.cloned.1.call-start = ((), (), s32[]{:S(2)}) async-start(), calls=%async_computation.6 | async-start | bytes 1064960 | tf_op jit(solution)/shard_map/all_gather | solution.py:95
  8.7 281.6 %all-reduce.6.cloned.1.call-start = ((), (), s32[]{:S(2)}) async-start(), calls=%async_computation.7 | async-start | bytes 5505024 | tf_op jit(solution)/shard_map/psum | solution.py:83
  194.5 1.7 copy-start.9
  197.5 0.9 copy-start.13
  197.5 1.1 copy-start.14
  197.5 13.0 %copy-start.11 = (bf16[2,512,256]{2,1,0:T(8,128)(2,1)S(1)}, bf16[2,512,256]{2,1,0:T(8,128)(2,1)}, u32[]{:S(2)}) copy-start(bf16[2,512,256]{2,1,0:T(8,128)(2,1)} %param.11) | copy-start | bytes 1572868
  197.6 13.6 %copy-start.12 = (bf16[128,512]{1,0:T(8,128)(2,1)S(1)}, bf16[128,512]{1,0:T(8,128)(2,1)}, u32[]{:S(2)}) copy-start(bf16[128,512]{1,0:T(8,128)(2,1)} %param.7) | copy-start | bytes 393220
  197.6 295.0 %all-reduce.4.cloned.1.call-start = ((), (), s32[]{:S(2)}) async-start(), calls=%async_computation.4 | async-start | bytes 2097152 | tf_op jit(solution)/shard_map/psum | solution.py:136
  210.7 79.5 %copy-start.1 = (bf16[2,512,256]{1,2,0:T(8,128)(2,1)}, bf16[2,512,256]{1,2,0:T(8,128)(2,1)S(1)}, u32[]{:S(2)}) copy-start(bf16[2,512,256]{1,2,0:T(8,128)(2,1)S(1)} %copy.64) | copy-start | bytes 1572868
  290.3 2.4 copy-start.10
  293.2 0.8 copy-start.4
  293.2 0.9 copy-start.6
  293.3 1.5 copy-start.3
  297.7 458.9 %reduce-scatter.3.cloned.1.call-start = ((), (), s32[]{:S(2)}) async-start(), calls=%async_computation.2 | async-start | bytes 2129920 | tf_op jit(solution)/shard_map/reduce_scatter | solution.py:22
  297.8 1.0 copy-start.8
  298.7 2.0 copy-start.2
  300.5 719.1 %reduce-scatter.5.cloned.1.call-start = ((), (), s32[]{:S(2)}) async-start(), calls=%async_computation.3 | async-start | bytes 2129920 | tf_op jit(solution)/shard_map/reduce_scatter | solution.py:22
  300.8 1.5 copy-start.5
  300.8 1.5 copy-start.7
Sparse Core Ops, SparseCore 0:
  10.2 35.8 all-gather.5
  48.1 146.3 all-gather.7
  197.7 92.5 all-reduce.5
  297.8 194.6 all-reduce.3
  495.2 261.4 reduce-scatter.2
  759.5 260.0 reduce-scatter.4
where the time goes:
time: 1030 us
  waiting for transfers between devices  922 us (90%)
  blocking collectives  55.6 us (5%)
  local copies, waits for them, and re-layouts  15.7 us (2%)
  between operations  14.4 us (1%)
  matrix products  13.6 us (1%)
    reduce_scatter x2, waiting for transfers between devices, settle_stationary(): lax.psum_scatter(block_sums, ('dp', 'hidden'), scatter_dimension=0, tiled...  523 us
    psum x1, waiting for transfers between devices, local(): adapter_input_gradient = lax.psum(input_map_piece, ('dp', 'hidden'))  182 us
    all_gather x1, waiting for transfers between devices, local(): lax.all_gather(cotangent[None], ('dp', 'hidden'), axis=0, tiled=True)  145 us
    all_gather x1, waiting for transfers between devices, local(): lax.all_gather(token_row_blocks, 'dp', axis=0, tiled=True)  37.3 us
    psum x1, waiting for transfers between devices, local(): frozen_sums = lax.psum(frozen_sums, 'width')  33.3 us
    psum x1, blocking collectives, local(): low_part = lax.psum(low_part, 'width')  28.9 us
  transfers between devices with their start and end apart: 6, of which 6 were waited for; matrix products, arithmetic and copies ran while one was open for 2% of the time, Pallas kernels for 0%

commit v1 on v0

v1 whole, which is shorter than its diff:
```python
import functools

import jax
import jax.numpy as jnp
from jax import lax
from jax.experimental import pallas as pl
from jax.experimental.pallas import tpu as pltpu
from jax.sharding import PartitionSpec as P

JOB_COUNT = 16
ADAPTER_RANK = 16
JOB_COLS = JOB_COUNT * ADAPTER_RANK
JOB_ROWS = 128
SCALE = 0.5
F32 = jnp.float32
BF16 = jnp.bfloat16

NX, NYLO, NYHI, NCORE, NZ = 4, 2, 4, 2, 8
NY = NYLO * NYHI
PIECE = 64
FEAT = NX * NYLO * PIECE
TOK = NYHI * NCORE * JOB_ROWS
HID = 224
LOW = 2 * ADAPTER_RANK
ROWS = 3 * HID + LOW
HALF = ROWS // 2


def mm(a, b):
    return jnp.dot(a, b, preferred_element_type=F32)


def mm_nt(a, b):
    return lax.dot_general(a, b, (((1,), (1,)), ((), ())), preferred_element_type=F32)


def kernel(
    tok_ref, job_ref, gu_ref, dn_ref, a_ref, b_ref, cot_ref,
    mixed_ref, ig_ref, ga_ref, gb_ref,
    xc, jobs, tok_t, w1t, dnt, at, bt,
    part, send_r, send_l, recv_r, recv_l, held,
    outp, core_in, x_out, x_in, y_out, y_in,
    b_core_out, b_core_in, b_x_out, b_x_in, b_y_out, b_y_in, inner,
    ag_y_s, ag_y_r, job_y_s, job_y_r, ag_x_s, ag_x_r, ag_c_s, ag_c_r,
    rs_s, rs_r, zg_s, zg_r, oc_s, oc_r, ox_s, ox_r, oy_s, oy_r,
    bc_s, bc_r, bx_s, bx_r, by_s, by_r, bz_s, bz_r,
):
    dp = lax.axis_index("dp")
    z = lax.axis_index("width")
    hid = lax.axis_index("hidden")
    yhi, core = dp // NCORE, dp % NCORE
    ylo, x = hid // NX, hid % NX
    y = yhi * NYLO + ylo
    right, left = (z + 1) % NZ, (z + NZ - 1) % NZ
    sibling = (yhi * NCORE + 1 - core, z, hid)

    def y_dev(other):
        return ((other // NYLO) * NCORE + core, z, (other % NYLO) * NX + x)

    def x_dev(other):
        return (dp, z, ylo * NX + other)

    def z_dev(other):
        return (dp, other, hid)

    def send(src, dst, s, r, dev):
        copy = pltpu.make_async_remote_copy(
            src_ref=src, dst_ref=dst, send_sem=s, recv_sem=r,
            device_id=dev, device_id_type=pl.DeviceIdType.MESH,
        )
        copy.start()
        sent.append(copy)

    def arrived(dst, s, r):
        pltpu.make_async_remote_copy(
            src_ref=dst, dst_ref=dst, send_sem=s, recv_sem=r,
            device_id=sibling, device_id_type=pl.DeviceIdType.MESH,
        ).wait_recv()

    sent = []
    barrier = pltpu.get_barrier_semaphore()
    partners = [sibling]
    partners += [y_dev((y + k) % NY) for k in range(1, NY)]
    partners += [x_dev((x + k) % NX) for k in range(1, NX)]
    partners += [z_dev((z + k) % NZ) for k in range(1, NZ)]
    for dev in partners:
        pl.semaphore_signal(barrier, inc=1, device_id=dev, device_id_type=pl.DeviceIdType.MESH)

    own_lanes = pl.ds(pl.multiple_of((core * NYHI + yhi) * JOB_ROWS, JOB_ROWS), JOB_ROWS)
    core_lanes = pl.ds(pl.multiple_of(core * (TOK // 2), TOK // 2), TOK // 2)
    peer_lanes = pl.ds(pl.multiple_of((1 - core) * (TOK // 2), TOK // 2), TOK // 2)
    tok_t[...] = tok_ref[...].T.reshape(NYLO, NX, PIECE, JOB_ROWS)
    xc[0, ylo, x, :, own_lanes] = tok_t[ylo, x]
    xc[1, ylo, x, :, own_lanes] = cot_ref[...].astype(F32).T.astype(BF16)
    jobs[:, own_lanes] = jnp.broadcast_to(job_ref[...].astype(F32), (16, JOB_ROWS)).astype(BF16)
    pl.semaphore_wait(barrier, len(partners))

    def lanes_of(other):
        return pl.ds(pl.multiple_of((core * NYHI + other // NYLO) * JOB_ROWS, JOB_ROWS), JOB_ROWS)

    own_piece = xc.at[:, ylo, x, :, own_lanes]
    own_jobs = jobs.at[:, own_lanes]
    for k in range(1, NY):
        dev = y_dev((y + k) % NY)
        send(own_piece, own_piece, ag_y_s.at[k - 1], ag_y_r.at[k - 1], dev)
    for k in range(1, NYHI):
        dev = y_dev((y + NYLO * k) % NY)
        send(own_jobs, own_jobs, job_y_s.at[k - 1], job_y_r.at[k - 1], dev)
    for k in range(2):
        w1t[k * HID:(k + 1) * HID, :] = gu_ref[k].T
        at[k * JOB_COLS:(k + 1) * JOB_COLS, :] = a_ref[k].T
        bt[k] = b_ref[k].T
    dnt[...] = dn_ref[...].T
    for k in range(1, NY):
        other = (y + NY - k) % NY
        arrived(xc.at[:, other % NYLO, x, :, lanes_of(other)], ag_y_s.at[k - 1], ag_y_r.at[k - 1])
    for k in range(1, NYHI):
        other = (y + NY - NYLO * k) % NY
        arrived(jobs.at[:, lanes_of(other)], job_y_s.at[k - 1], job_y_r.at[k - 1])

    mine = xc.at[:, :, x, :, core_lanes]
    for k in range(1, NX):
        send(mine, mine, ag_x_s.at[k - 1], ag_x_r.at[k - 1], x_dev((x + k) % NX))
    send(jobs.at[:, core_lanes], jobs.at[:, core_lanes], ag_c_s.at[1], ag_c_r.at[1], sibling)
    for k in range(1, NX):
        arrived(xc.at[:, :, (x + NX - k) % NX, :, core_lanes], ag_x_s.at[k - 1], ag_x_r.at[k - 1])
    half = xc.at[:, :, :, :, core_lanes]
    send(half, half, ag_c_s.at[0], ag_c_r.at[0], sibling)
    arrived(jobs.at[:, peer_lanes], ag_c_s.at[1], ag_c_r.at[1])
    arrived(xc.at[:, :, :, :, peer_lanes], ag_c_s.at[0], ag_c_r.at[0])

    def job_mask(lanes, width):
        row = jobs[:, lanes].astype(F32)[0:1]
        col = lax.broadcasted_iota(jnp.int32, (JOB_COLS, width), 0) // ADAPTER_RANK
        return col.astype(F32) == row

    @pl.loop(0, TOK // 256)
    def _(q):
        lanes = pl.ds(pl.multiple_of(q * 256, 256), 256)
        rows = xc[0, :, :, :, lanes].reshape(FEAT, 256)
        grads = xc[1, :, :, :, lanes].reshape(FEAT, 256)
        pre = mm(w1t[...], rows)
        back = mm(dn_ref[...], grads)
        mask = job_mask(lanes, 256)
        low = mm(at[...], rows)
        lows = []
        for k in range(2):
            picked = jnp.where(mask, low[k * JOB_COLS:(k + 1) * JOB_COLS], 0.0)
            lows.append(picked.reshape(JOB_COUNT, ADAPTER_RANK, 256).sum(0))
        for i in range(2):
            cut = slice(i * 128, (i + 1) * 128)
            part[2 * q + i, 0:2 * HID, :] = pre[:, cut]
            part[2 * q + i, 2 * HID:3 * HID, :] = back[:, cut]
            for k in range(2):
                at_row = 3 * HID + k * ADAPTER_RANK
                part[2 * q + i, at_row:at_row + ADAPTER_RANK, :] = lows[k][:, cut]

    first, second = pl.ds(0, HALF), pl.ds(HALF, HALF)
    far = (z + NZ // 2) % NZ
    send_r[0, first, :] = part[far, first, :].astype(BF16)
    send(send_r.at[0, first], recv_r.at[0, first], rs_s.at[0, 0], rs_r.at[0, 0], z_dev(right))
    send_l[0, second, :] = part[far, second, :].astype(BF16)
    send(send_l.at[0, second], recv_l.at[0, second], rs_s.at[1, 0], rs_r.at[1, 0], z_dev(left))
    for t in range(1, 4):
        block_r, block_l = (z + 4 - t) % NZ, (z + 4 + t) % NZ
        if t == 1:
            send_r[t, second, :] = part[block_r, second, :].astype(BF16)
            arrived(recv_r.at[0, first], rs_s.at[0, 0], rs_r.at[0, 0])
            send_r[t, first, :] = (part[block_r, first, :] + recv_r[0, first, :].astype(F32)).astype(BF16)
        else:
            arrived(recv_r.at[t - 1], rs_s.at[0, t - 1], rs_r.at[0, t - 1])
            send_r[t] = (part[block_r] + recv_r[t - 1].astype(F32)).astype(BF16)
        send(send_r.at[t], recv_r.at[t], rs_s.at[0, t], rs_r.at[0, t], z_dev(right))
        if t == 1:
            send_l[t, first, :] = part[block_l, first, :].astype(BF16)
            arrived(recv_l.at[0, second], rs_s.at[1, 0], rs_r.at[1, 0])
            send_l[t, second, :] = (part[block_l, second, :] + recv_l[0, second, :].astype(F32)).astype(BF16)
        else:
            arrived(recv_l.at[t - 1], rs_s.at[1, t - 1], rs_r.at[1, t - 1])
            send_l[t] = (part[block_l] + recv_l[t - 1].astype(F32)).astype(BF16)
        send(send_l.at[t], recv_l.at[t], rs_s.at[1, t], rs_r.at[1, t], z_dev(left))
    arrived(recv_r.at[3], rs_s.at[0, 3], rs_r.at[0, 3])
    arrived(recv_l.at[3], rs_s.at[1, 3], rs_r.at[1, 3])
    total = part[z] + recv_r[3].astype(F32) + recv_l[3].astype(F32)

    mask = job_mask(pl.ds(pl.multiple_of(z * JOB_ROWS, JOB_ROWS), JOB_ROWS), JOB_ROWS)
    pre_act = []
    for k in range(2):
        low = total[3 * HID + k * ADAPTER_RANK:3 * HID + (k + 1) * ADAPTER_RANK]
        wide = jnp.where(mask, jnp.concatenate([low] * JOB_COUNT, axis=0), 0.0).astype(BF16)
        pre_act.append(total[k * HID:(k + 1) * HID] + SCALE * mm(bt[k], wide))
    gate, up = pre_act
    back = total[2 * HID:3 * HID]
    sig = jax.nn.sigmoid(gate)
    silu = gate * sig
    grads = [
        (back * up * sig * (1.0 + gate * (1.0 - sig))).astype(BF16),
        (back * silu).astype(BF16),
    ]
    held[z, 0:HID, :] = (silu * up).astype(BF16)
    held[z, HID:2 * HID, :] = grads[0]
    held[z, 2 * HID:3 * HID, :] = grads[1]
    held[z, 3 * HID:, :] = total[3 * HID:].astype(BF16)
    send(held.at[z], held.at[z], zg_s.at[0, 0], zg_r.at[0, 0], z_dev(right))
    send(held.at[z], held.at[z], zg_s.at[1, 0], zg_r.at[1, 0], z_dev(left))
    for k in range(2):
        wide = jnp.where(mask, mm(b_ref[k], grads[k]), 0.0)
        b_core_out[k * ADAPTER_RANK:(k + 1) * ADAPTER_RANK, :] = SCALE * wide.reshape(
            JOB_COUNT, ADAPTER_RANK, JOB_ROWS
        ).sum(0)
    send(b_core_out, b_core_in, bc_s.at[0], bc_r.at[0], sibling)

    def outputs_of(blocks):
        def rows_of(lo, hi):
            return jnp.concatenate([held[p, lo:hi, :] for p in blocks], axis=1)

        out = mm(dnt[...], rows_of(0, HID))
        grad = mm(gu_ref[0], rows_of(HID, 2 * HID)) + mm(gu_ref[1], rows_of(2 * HID, 3 * HID))
        for i, p in enumerate(blocks):
            cut = slice(i * 128, (i + 1) * 128)
            outp[p, 0] = out[:, cut].astype(BF16).reshape(NYLO, NX, PIECE, JOB_ROWS)
            outp[p, 1] = grad[:, cut].astype(BF16).reshape(NYLO, NX, PIECE, JOB_ROWS)

    outputs_of([z])
    for t in range(1, 4):
        block_r, block_l = (z + NZ - t) % NZ, (z + t) % NZ
        arrived(held.at[block_r], zg_s.at[0, t - 1], zg_r.at[0, t - 1])
        piece = held.at[block_r, first] if t == 3 else held.at[block_r]
        send(piece, piece, zg_s.at[0, t], zg_r.at[0, t], z_dev(right))
        arrived(held.at[block_l], zg_s.at[1, t - 1], zg_r.at[1, t - 1])
        piece = held.at[block_l, second] if t == 3 else held.at[block_l]
        send(piece, piece, zg_s.at[1, t], zg_r.at[1, t], z_dev(left))
        if t == 1:
            arrived(b_core_in, bc_s.at[0], bc_r.at[0])
            b_x_out[...] = b_core_out[...] + b_core_in[...]
            for k in range(1, NX):
                send(b_x_out, b_x_in.at[k - 1], bx_s.at[k - 1], bx_r.at[k - 1], x_dev((x + k) % NX))
        elif t == 2:
            both = b_x_out[...]
            for k in range(1, NX):
                arrived(b_x_in.at[k - 1], bx_s.at[k - 1], bx_r.at[k - 1])
                both = both + b_x_in[k - 1]
            b_y_out[...] = both
            for k in range(1, NY):
                send(b_y_out, b_y_in.at[k - 1], by_s.at[k - 1], by_r.at[k - 1], y_dev((y + k) % NY))
        else:
            both = b_y_out[...]
            for k in range(1, NY):
                arrived(b_y_in.at[k - 1], by_s.at[k - 1], by_r.at[k - 1])
                both = both + b_y_in[k - 1]
            inner[z] = both
            for k in range(1, NZ):
                send(inner.at[z], inner.at[z], bz_s.at[k - 1], bz_r.at[k - 1], z_dev((z + k) % NZ))
        outputs_of([block_r, block_l])
    arrived(held.at[far, first], zg_s.at[0, 3], zg_r.at[0, 3])
    arrived(held.at[far, second], zg_s.at[1, 3], zg_r.at[1, 3])
    outputs_of([far])

    peer_blocks = pl.ds((1 - core) * NYHI, NYHI)
    send(outp.at[peer_blocks], core_in, oc_s.at[0], oc_r.at[0], sibling)
    for k in range(2):
        acc = jnp.zeros((JOB_COLS, HID), F32)
        for q in range(TOK // 256):
            at_row = 3 * HID + k * ADAPTER_RANK
            low = jnp.concatenate(
                [held[2 * q + i, at_row:at_row + ADAPTER_RANK, :] for i in range(2)], axis=1
            ).astype(F32)
            wide = jnp.where(
                job_mask(pl.ds(q * 256, 256), 256), jnp.concatenate([low] * JOB_COUNT, axis=0), 0.0
            ).astype(BF16)
            grad = jnp.concatenate(
                [held[2 * q + i, (1 + k) * HID:(2 + k) * HID, :] for i in range(2)], axis=1
            )
            acc = acc + mm_nt(wide, grad)
        gb_ref[k] = SCALE * acc
    arrived(core_in, oc_s.at[0], oc_r.at[0])
    for i in range(NYHI):
        x_out[i] = (outp[core * NYHI + i].astype(F32) + core_in[i].astype(F32)).astype(BF16)
    for k in range(1, NX):
        other = (x + k) % NX
        send(x_out.at[:, :, :, other], x_in.at[k - 1], ox_s.at[k - 1], ox_r.at[k - 1], x_dev(other))
    for k in range(1, NZ):
        arrived(inner.at[(z + NZ - k) % NZ], bz_s.at[k - 1], bz_r.at[k - 1])

    def wide_inner(k, p, mask):
        part_inner = inner[p, k * ADAPTER_RANK:(k + 1) * ADAPTER_RANK, :]
        wide = jnp.where(mask, jnp.concatenate([part_inner] * JOB_COUNT, axis=0), 0.0)
        hi = wide.astype(BF16)
        return hi, (wide - hi.astype(F32)).astype(BF16)

    for k in range(2):
        acc = jnp.zeros((FEAT, JOB_COLS), F32)
        for q in range(TOK // 256):
            rows = xc[0, :, :, :, q * 256:(q + 1) * 256].reshape(FEAT, 256)
            parts = []
            for p in (2 * q, 2 * q + 1):
                parts.append(wide_inner(k, p, job_mask(pl.ds(p * 128, 128), 128)))
            acc = acc + mm_nt(rows, jnp.concatenate([parts[0][0], parts[1][0]], axis=1))
            acc = acc + mm_nt(rows, jnp.concatenate([parts[0][1], parts[1][1]], axis=1))
        ga_ref[k] = acc
    for k in range(1, NX):
        arrived(x_in.at[k - 1], ox_s.at[k - 1], ox_r.at[k - 1])
    for i in range(NYHI):
        both = x_out[i, :, :, x].astype(F32)
        for k in range(1, NX):
            both = both + x_in[k - 1, i].astype(F32)
        y_out[i] = both.astype(BF16)
    for k in range(1, NY):
        other = (y + k) % NY
        send(y_out.at[other // NYLO, :, other % NYLO], y_in.at[k - 1],
             oy_s.at[k - 1], oy_r.at[k - 1], y_dev(other))
    own_block = core * NYHI + yhi
    mask = job_mask(own_lanes, JOB_ROWS)
    extra = jnp.zeros((PIECE, JOB_ROWS), F32)
    for k in range(2):
        cols = a_ref[k, pl.ds(pl.multiple_of(hid * PIECE, PIECE), PIECE), :]
        for wide in wide_inner(k, own_block, mask):
            extra = extra + mm(cols, wide)
    out = y_out[yhi, 0, ylo].astype(F32)
    grad = y_out[yhi, 1, ylo].astype(F32) + extra
    for k in range(1, NY):
        arrived(y_in.at[k - 1], oy_s.at[k - 1], oy_r.at[k - 1])
        out = out + y_in[k - 1, 0].astype(F32)
        grad = grad + y_in[k - 1, 1].astype(F32)
    mixed_ref[...] = out.T.astype(BF16)
    ig_ref[...] = grad.T.astype(BF16)
    for copy in sent:
        copy.wait_send()


def local(tokens, token_job_index, gate_up, down, adapter_in, adapter_out, cotangent):
    vmem = pl.BlockSpec(memory_space=pltpu.VMEM)
    dma = lambda *shape: pltpu.SemaphoreType.DMA(shape)
    buf = pltpu.VMEM
    tile = (PIECE, JOB_ROWS)
    sems = [
        NY - 1, NY - 1, NYHI - 1, NYHI - 1, NX - 1, NX - 1, 2, 2,
        (2, 4), (2, 4), (2, 4), (2, 4), 1, 1, NX - 1, NX - 1, NY - 1, NY - 1,
        1, 1, NX - 1, NX - 1, NY - 1, NY - 1, NZ - 1, NZ - 1,
    ]
    return pl.pallas_call(
        kernel,
        out_shape=[
            jax.ShapeDtypeStruct((JOB_ROWS, PIECE), BF16),
            jax.ShapeDtypeStruct((JOB_ROWS, PIECE), BF16),
            jax.ShapeDtypeStruct((2, FEAT, JOB_COLS), F32),
            jax.ShapeDtypeStruct((2, JOB_COLS, HID), F32),
        ],
        in_specs=[vmem] * 7,
        out_specs=[vmem] * 4,
        scratch_shapes=[
            buf((2, NYLO, NX, PIECE, TOK), BF16),
            buf((16, TOK), BF16),
            buf((NYLO, NX) + tile, BF16),
            buf((2 * HID, FEAT), BF16),
            buf((FEAT, HID), BF16),
            buf((2 * JOB_COLS, FEAT), BF16),
            buf((2, HID, JOB_COLS), BF16),
            buf((NZ, ROWS, JOB_ROWS), F32),
            buf((4, ROWS, JOB_ROWS), BF16),
            buf((4, ROWS, JOB_ROWS), BF16),
            buf((4, ROWS, JOB_ROWS), BF16),
            buf((4, ROWS, JOB_ROWS), BF16),
            buf((NZ, ROWS, JOB_ROWS), BF16),
            buf((NZ, 2, NYLO, NX) + tile, BF16),
            buf((NYHI, 2, NYLO, NX) + tile, BF16),
            buf((NYHI, 2, NYLO, NX) + tile, BF16),
            buf((NX - 1, NYHI, 2, NYLO) + tile, BF16),
            buf((NYHI, 2, NYLO) + tile, BF16),
            buf((NY - 1, 2) + tile, BF16),
            buf((LOW, JOB_ROWS), F32),
            buf((LOW, JOB_ROWS), F32),
            buf((LOW, JOB_ROWS), F32),
            buf((NX - 1, LOW, JOB_ROWS), F32),
            buf((LOW, JOB_ROWS), F32),
            buf((NY - 1, LOW, JOB_ROWS), F32),
            buf((NZ, LOW, JOB_ROWS), F32),
        ] + [dma(*s) if isinstance(s, tuple) else dma(s) for s in sems],
        compiler_params=pltpu.CompilerParams(
            collective_id=0, has_side_effects=True, vmem_limit_bytes=44 * 1024 * 1024
        ),
    )(
        tokens, token_job_index.reshape(1, JOB_ROWS), gate_up, down,
        adapter_in, adapter_out, cotangent,
    )


def solution(mesh):
    return jax.shard_map(
        local,
        mesh=mesh,
        in_specs=(
            P("dp", "width"),
            P("dp"),
            P(None, "width", ("dp", "hidden")),
            P(("dp", "hidden"), "width"),
            P(None, "width", None),
            P(None, None, ("dp", "hidden")),
            P("dp", ("width", "hidden")),
        ),
        out_specs=(
            P("dp", ("width", "hidden")),
            P("dp", ("width", "hidden")),
            P(None, "width", None),
            P(None, None, ("dp", "hidden")),
        ),
        check_vma=False,
    )
```

time: 1030 us -> 116 us (0.11)
  the two profiles are of different devices: /device:TPU:64 before, /device:TPU:65 now
where the time goes in v1:
time: 116 us
  Pallas kernels  109 us (94%)
  local copies, waits for them, and re-layouts  6.38 us (6%)
    pallas_call x1, Pallas kernels, local(): pl.pallas_call(kernel, out_shape=[jax.ShapeDtypeStruct((JOB_ROWS, PIECE),...  109 us
    unnamed x14, local copies, waits for them, and re-layouts  4.03 us
    pallas_call x3, local copies, waits for them, and re-layouts, local(): pl.pallas_call(kernel, out_shape=[jax.ShapeDtypeStruct((JOB_ROWS, PIECE),...  2.35 us

profile of v1, /device:TPU:65, one launch (start us, length us, event | category | flops | bytes accessed | tf_op | source)
XLA Modules:
  0.0 115.6 jit_solution(7791630703603016035)
XLA Ops:
  0.6 0.0 copy-start.4
  0.6 0.9 copy.13.cot_ref
  1.5 1.1 copy.12.b_ref
  2.6 0.0 copy-done.4
  2.6 0.0 copy-start
  2.6 0.0 copy-start.1
  2.6 0.0 copy-start.2
  2.7 0.0 copy-start.3
  2.7 0.2 copy.11.gu_ref
  2.9 0.8 copy-done
  3.7 0.1 copy-done.1
  3.7 0.0 copy-done.2
  3.8 0.0 copy-done.3
  3.8 108.5 %shard_map.102 = (bf16[128,64]{1,0:T(8,128)(2,1)S(1)}, bf16[128,64]{1,0:T(8,128)(2,1)S(1)}, f32[2,512,256]{2,1,0:T(8,128)S(1)}, f32[2,256,224]{2,1,0:T(8,128)S(1)}) custom-call(bf16[128,512]{1,0:T(8,128)(2,1)S(1)} %copy-done.2, s32[1,128]{1,0:T(1,128)S(1)} %bitcast.1, bf16[2,512,224]{2,1,0:T(8,128)(2,1)S(1)} %copy.11.gu_ref, bf16[224,512]{1,0:T(8,128)(2,1)S(1)} %copy-done.1, ...), custom_call_target="tpu_custom_call" | custom-call | tf_op jit(solution)/shard_map/pallas_call | solution.py:341
  112.3 0.7 copy.14
  113.0 0.7 copy.15
  113.7 1.0 copy.16
  114.7 1.0 copy.18
Async XLA Ops:
  0.6 2.0 %copy-start.4 = (bf16[2,512,224]{1,2,0:T(8,128)(2,1)S(1)}, bf16[2,512,224]{1,2,0:T(8,128)(2,1)}, u32[]{:S(2)}) copy-start(bf16[2,512,224]{1,2,0:T(8,128)(2,1)} %param.9) | copy-start | bytes 1376260
  2.6 1.0 copy-start
  2.6 1.1 copy-start.1
  2.6 1.1 copy-start.2
  2.7 1.1 copy-start.3

commit v2 on v1

v2 whole, which is shorter than its diff:
```python
import jax
import jax.numpy as jnp
from jax import lax
from jax.experimental import pallas as pl
from jax.experimental.pallas import tpu as pltpu
from jax.sharding import PartitionSpec as P

JOB_COUNT = 16
ADAPTER_RANK = 16
JOB_COLS = JOB_COUNT * ADAPTER_RANK
JOB_ROWS = 128
SCALE = 0.5
F32 = jnp.float32
BF16 = jnp.bfloat16

NX, NYLO, NYHI, NCORE, NZ = 4, 2, 4, 2, 8
NY = NYLO * NYHI
PIECE = 64
FEAT = NX * NYLO * PIECE
HID = 224
LOW = 2 * ADAPTER_RANK
SUMS = ((0, 240), (240, 480), (480, 592), (592, 704))
LOW_AT, BACK_AT = 2 * HID, 2 * HID + LOW
PARTS = ((0, 128), (128, 256), (256, 480), (480, 704))
HLOW_AT, GRAD_AT = HID, HID + LOW
ROWS = 3 * HID + LOW


def mm(a, b):
    return jnp.dot(a, b, preferred_element_type=F32)


def mm_nt(a, b):
    return lax.dot_general(a, b, (((1,), (1,)), ((), ())), preferred_element_type=F32)


def kernel(
    tok_hbm, job_hbm, gut_hbm, dn_hbm, a_hbm, bt_hbm, cot_hbm,
    mixed_hbm, ig_hbm, ga_hbm, gb_hbm,
    tok_ref, job_ref, gut_ref, dn_ref, a_ref, bt_ref,
    mixed_ref, ig_ref, ga_ref, gb_ref,
    xc, jobs, gu, dnt, at, bn,
    part, ring_out, ring_in, held,
    outp, core_in, x_out, x_in, y_out, y_in, fin, fin_in,
    b_core_out, b_core_in, b_x_out, b_x_in, b_y_out, b_y_in, inner,
    ty_s, ty_r, tx_s, tx_r, tf_s, tf_r, tc_s, tc_r, jy_s, jy_r, jc_s, jc_r,
    rs_s, rs_r, zg_s, zg_r, oc_s, oc_r, ox_s, ox_r, oy_s, oy_r, of_s, of_r,
    bc_s, bc_r, bx_s, bx_r, by_s, by_r, bz_s, bz_r, load_s, store_s,
):
    dp = lax.axis_index("dp")
    z = lax.axis_index("width")
    hid = lax.axis_index("hidden")
    yhi, core = dp // NCORE, dp % NCORE
    ylo, x = hid // NX, hid % NX
    y = yhi * NYLO + ylo
    sibling = (yhi * NCORE + 1 - core, z, hid)
    far = (z + NZ // 2) % NZ

    def y_dev(other):
        return ((other // NYLO) * NCORE + core, z, (other % NYLO) * NX + x)

    def x_dev(other):
        return (dp, z, ylo * NX + other)

    def z_dev(other):
        return (dp, other, hid)

    next_dev = (z_dev((z + 1) % NZ), z_dev((z + NZ - 1) % NZ))
    sent = []

    def send(src, dst, s, r, dev):
        copy = pltpu.make_async_remote_copy(
            src_ref=src, dst_ref=dst, send_sem=s, recv_sem=r,
            device_id=dev, device_id_type=pl.DeviceIdType.MESH,
        )
        copy.start()
        sent.append(copy)

    def arrived(dst, s, r):
        pltpu.make_async_remote_copy(
            src_ref=dst, dst_ref=dst, send_sem=s, recv_sem=r,
            device_id=sibling, device_id_type=pl.DeviceIdType.MESH,
        ).wait_recv()

    own_cot = xc.at[yhi, core, ylo, x, 1]
    loads = {}
    for i, (src, dst) in enumerate((
        (tok_hbm, tok_ref), (cot_hbm, own_cot), (job_hbm, job_ref), (a_hbm, a_ref),
        (gut_hbm, gut_ref), (dn_hbm, dn_ref), (bt_hbm, bt_ref),
    )):
        loads[i] = pltpu.make_async_copy(src, dst, load_s.at[i])
        loads[i].start()
    stores = []

    def store(i, src, dst):
        copy = pltpu.make_async_copy(src, dst, store_s.at[i])
        copy.start()
        stores.append(copy)

    barrier = pltpu.get_barrier_semaphore()
    partners = [sibling]
    partners += [y_dev((y + k) % NY) for k in range(1, NY)]
    partners += [x_dev((x + k) % NX) for k in range(1, NX)]
    partners += [z_dev((z + k) % NZ) for k in range(1, NZ)]
    for dev in partners:
        pl.semaphore_signal(barrier, inc=1, device_id=dev, device_id_type=pl.DeviceIdType.MESH)
    eye = (
        lax.broadcasted_iota(jnp.int32, (256, 256), 0)
        == lax.broadcasted_iota(jnp.int32, (256, 256), 1)
    ).astype(F32).astype(BF16)

    def turned(ref):
        cols = ref.shape[1]
        return jnp.concatenate(
            [mm_nt(eye, ref[:, i:i + 256]) for i in range(0, cols, 256)], axis=0
        ).astype(BF16)

    loads[0].wait()
    xc[yhi, core, :, :, 0] = turned(tok_ref).reshape(NYLO, NX, PIECE, JOB_ROWS)
    loads[1].wait()
    loads[2].wait()
    jobs[yhi, core] = jnp.broadcast_to(job_ref[...].astype(F32), (16, JOB_ROWS)).astype(BF16)
    pl.semaphore_wait(barrier, len(partners))

    def piece(k, src, low, at_x):
        view = xc.at[src, core, low, at_x]
        return view if k else xc.at[src, core, low, at_x, 1]

    both_low = pl.ds(0, NYLO)
    order = (0, 1, 3, 2)
    source = [(yhi + NYHI - k) % NYHI for k in range(NYHI)]
    own = xc.at[yhi, core, ylo, x]
    send(own_cot, own_cot, ty_s.at[0, 0], ty_r.at[0, 0], y_dev(yhi * NYLO + 1 - ylo))
    for k in order[1:]:
        for low in range(NYLO):
            dev = y_dev(((yhi + k) % NYHI) * NYLO + low)
            send(own, own, ty_s.at[k, low], ty_r.at[k, ylo], dev)
    own = xc.at[yhi, core, :, :, 0]
    send(own, own, tc_s.at[NYHI], tc_r.at[NYHI], sibling)
    own = jobs.at[yhi, core]
    for k in range(1, NYHI):
        dev = y_dev(((yhi + k) % NYHI) * NYLO + ylo)
        send(own, own, jy_s.at[k - 1], jy_r.at[k - 1], dev)
    loads[3].wait()
    for k in range(2):
        at[k * JOB_COLS:(k + 1) * JOB_COLS, :] = turned(a_ref.at[k])
    x_next = (x_dev((x + 1) % NX), x_dev((x + NX - 1) % NX))
    x_from = ((x + NX - 1) % NX, (x + 1) % NX)
    for k in order:
        src = source[k]
        if k == 0:
            arrived(piece(0, src, 1 - ylo, x), ty_s.at[0, 0], ty_r.at[0, 0])
        else:
            for low in range(NYLO):
                arrived(piece(k, src, low, x), ty_s.at[k, low], ty_r.at[k, low])
        for way in range(2):
            own = piece(k, src, both_low, x)
            send(own, own, tx_s.at[k, way], tx_r.at[k, way], x_next[way])
    for k in range(1, NYHI):
        arrived(jobs.at[source[k], core], jy_s.at[k - 1], jy_r.at[k - 1])
    send(jobs.at[:, core], jobs.at[:, core], jc_s.at[0], jc_r.at[0], sibling)
    for i in range(4, 7):
        loads[i].wait()
    for k in range(2):
        gu[k] = turned(gut_ref.at[k])
        bn[k] = turned(bt_ref.at[k])
    dnt[...] = turned(dn_ref)
    for k in order:
        for way in range(2):
            arrived(piece(k, source[k], both_low, x_from[way]), tx_s.at[k, way], tx_r.at[k, way])
            onward = piece(k, source[k], way, x_from[way])
            send(onward, onward, tf_s.at[k, way], tf_r.at[k, way], x_next[way])
    for k in order:
        for way in range(2):
            across = piece(k, source[k], way, (x + 2) % NX)
            arrived(across, tf_s.at[k, way], tf_r.at[k, way])
        whole = xc.at[source[k], core] if k else xc.at[yhi, core, :, :, 1]
        send(whole, whole, tc_s.at[k], tc_r.at[k], sibling)
    arrived(jobs.at[:, 1 - core], jc_s.at[0], jc_r.at[0])
    arrived(xc.at[yhi, 1 - core, :, :, 0], tc_s.at[NYHI], tc_r.at[NYHI])
    for k in order:
        whole = xc.at[source[k], 1 - core] if k else xc.at[yhi, 1 - core, :, :, 1]
        arrived(whole, tc_s.at[k], tc_r.at[k])

    def wide_mask(row):
        row = row.astype(F32)[0:1]
        col = lax.broadcasted_iota(jnp.int32, (JOB_COLS, row.shape[1]), 0) // ADAPTER_RANK
        return col.astype(F32) == row

    def pair(kind, q):
        return jnp.concatenate(
            [xc[q, c, :, :, kind].reshape(FEAT, JOB_ROWS) for c in range(NCORE)], axis=1
        )

    def pair_mask(q):
        return wide_mask(jnp.concatenate([jobs[q, c] for c in range(NCORE)], axis=1))

    def forward_sums(q):
        rows = pair(0, q)
        mask = pair_mask(q)
        pre = [mm(gut_ref[k], rows) for k in range(2)]
        low = mm(at[...], rows)
        for k in range(2):
            picked = jnp.where(mask, low[k * JOB_COLS:(k + 1) * JOB_COLS], 0.0)
            picked = picked.reshape(JOB_COUNT, ADAPTER_RANK, 2 * JOB_ROWS).sum(0)
            low_at = LOW_AT + k * ADAPTER_RANK
            for c in range(NCORE):
                cut = slice(c * JOB_ROWS, (c + 1) * JOB_ROWS)
                part[NCORE * q + c, k * HID:(k + 1) * HID, :] = pre[k][:, cut]
                part[NCORE * q + c, low_at:low_at + ADAPTER_RANK, :] = picked[:, cut]

    def backward_sums(q):
        back = mm(dn_ref[...], pair(1, q))
        for c in range(NCORE):
            part[NCORE * q + c, BACK_AT:, :] = back[:, c * JOB_ROWS:(c + 1) * JOB_ROWS]

    def sum_step(t, chunks):
        ready = []
        for way in range(2):
            cuts = [c for c in chunks if t > 0 or c % 2 == way]
            cuts.sort(key=lambda c: c % 2 == way)
            ready.append(cuts)
        for cuts in zip(*ready):
            for way, c in enumerate(cuts):
                block = (z + 4 - t) % NZ if way == 0 else (z + 4 + t) % NZ
                lo, hi = SUMS[c]
                value = part[block, lo:hi, :]
                if t > 1 or (t == 1 and c % 2 == way):
                    before = ring_in.at[way, t - 1, lo:hi]
                    arrived(before, rs_s.at[way, t - 1, c], rs_r.at[way, t - 1, c])
                    value = value + before[...].astype(F32)
                ring_out[way, t, lo:hi, :] = value.astype(BF16)
                send(ring_out.at[way, t, lo:hi], ring_in.at[way, t, lo:hi],
                     rs_s.at[way, t, c], rs_r.at[way, t, c], next_dev[way])

    def sum_end(chunks):
        for c in chunks:
            lo, hi = SUMS[c]
            for way in range(2):
                arrived(ring_in.at[way, 3, lo:hi], rs_s.at[way, 3, c], rs_r.at[way, 3, c])
        lo, hi = SUMS[chunks[0]][0], SUMS[chunks[-1]][1]
        return part[z, lo:hi, :] + (
            ring_in[0, 3, lo:hi, :].astype(F32) + ring_in[1, 3, lo:hi, :].astype(F32)
        )

    def gather_step(t, chunks):
        for c in chunks:
            lo, hi = PARTS[c]
            for way in range(2):
                block = (z + NZ - t) % NZ if way == 0 else (z + t) % NZ
                piece = held.at[block, lo:hi]
                if t > 0:
                    arrived(piece, zg_s.at[way, t - 1, c], zg_r.at[way, t - 1, c])
                if t < 3 or c % 2 == way:
                    send(piece, piece, zg_s.at[way, t, c], zg_r.at[way, t, c], next_dev[way])

    def gather_end(chunks):
        for c in chunks:
            lo, hi = PARTS[c]
            arrived(held.at[far, lo:hi], zg_s.at[c % 2, 3, c], zg_r.at[c % 2, 3, c])

    def blocks_at(t):
        if t == 0 or t == 4:
            return [(z + t) % NZ]
        return [(z + NZ - t) % NZ, (z + t) % NZ]

    def held_rows(blocks, lo, hi):
        return jnp.concatenate([held[p, lo:hi, :] for p in blocks], axis=1)

    def slots(t):
        first = (0, 1, 3, 5, 7)[t]
        return [(first + i, p) for i, p in enumerate(blocks_at(t))]

    def core_stage(t):
        blocks = blocks_at(t)
        values = (
            mm(dnt[...], held_rows(blocks, 0, HID)),
            mm(gu[0], held_rows(blocks, GRAD_AT, GRAD_AT + HID))
            + mm(gu[1], held_rows(blocks, GRAD_AT + HID, ROWS)),
        )
        for j, (n, _) in enumerate(slots(t)):
            for i in range(2):
                cut = values[i][:, j * JOB_ROWS:(j + 1) * JOB_ROWS].astype(BF16)
                outp[n, i] = cut.reshape(NYLO, NX, PIECE, JOB_ROWS)
            send(outp.at[n, 1 - core], core_in.at[n], oc_s.at[n], oc_r.at[n], sibling)

    def x_stage(t):
        for n, _ in slots(t):
            arrived(core_in.at[n], oc_s.at[n], oc_r.at[n])
            x_out[n] = (outp[n, core].astype(F32) + core_in[n].astype(F32)).astype(BF16)
            for k in range(1, NX):
                other = (x + k) % NX
                send(x_out.at[n, :, other], x_in.at[n, k - 1],
                     ox_s.at[n, k - 1], ox_r.at[n, k - 1], x_dev(other))

    def y_copies(n, p):
        for low in range(NYLO):
            other = (p // NCORE) * NYLO + low
            k = (other + NY - y) % NY
            slot = (k + NY - 1) % NY
            yield k, pltpu.make_async_remote_copy(
                src_ref=y_out.at[n, low], dst_ref=y_in.at[p % NCORE, slot],
                send_sem=oy_s.at[n, low], recv_sem=oy_r.at[p % NCORE, slot],
                device_id=y_dev(other), device_id_type=pl.DeviceIdType.MESH,
            )

    def y_stage(t):
        for n, p in slots(t):
            both = x_out[n, :, x].astype(F32)
            for k in range(1, NX):
                arrived(x_in.at[n, k - 1], ox_s.at[n, k - 1], ox_r.at[n, k - 1])
                both = both + x_in[n, k - 1].astype(F32)
            y_out[n] = both.astype(BF16)
            for k, copy in y_copies(n, p):
                @pl.when(k != 0)
                def _(copy=copy):
                    copy.start()

            @pl.when(p // NCORE == yhi)
            def _(n=n, p=p):
                fin[p % NCORE] = y_out[n, ylo].astype(F32)

    forward, backward = (0, 1), (2, 3)
    every = forward + backward
    forward_sums(far // NCORE)
    backward_sums(far // NCORE)
    sum_step(0, every)

    @pl.loop(1, NYHI)
    def _(q):
        forward_sums((far // NCORE + q) % NYHI)
        backward_sums((far // NCORE + q) % NYHI)

    for t in range(1, 4):
        sum_step(t, every)

    total = sum_end(forward)
    mask = wide_mask(jobs[z // NCORE, z % NCORE])
    pre_act = []
    for k in range(2):
        low = total[LOW_AT + k * ADAPTER_RANK:LOW_AT + (k + 1) * ADAPTER_RANK]
        wide = jnp.where(mask, jnp.concatenate([low] * JOB_COUNT, axis=0), 0.0).astype(BF16)
        pre_act.append(total[k * HID:(k + 1) * HID] + SCALE * mm(bt_ref[k], wide))
    gate, up = pre_act
    sig = jax.nn.sigmoid(gate)
    silu = gate * sig
    held[z, 0:HID, :] = (silu * up).astype(BF16)
    held[z, HLOW_AT:GRAD_AT, :] = total[LOW_AT:BACK_AT].astype(BF16)
    gather_step(0, forward)
    back = sum_end(backward)
    grads = [
        (back * up * sig * (1.0 + gate * (1.0 - sig))).astype(BF16),
        (back * silu).astype(BF16),
    ]
    for k in range(2):
        held[z, GRAD_AT + k * HID:GRAD_AT + (k + 1) * HID, :] = grads[k]
    gather_step(0, backward)
    for k in range(2):
        wide = jnp.where(mask, mm(bn[k], grads[k]), 0.0)
        b_core_out[k * ADAPTER_RANK:(k + 1) * ADAPTER_RANK, :] = SCALE * wide.reshape(
            JOB_COUNT, ADAPTER_RANK, JOB_ROWS
        ).sum(0)
    send(b_core_out, b_core_in, bc_s.at[0], bc_r.at[0], sibling)
    core_stage(0)
    gather_step(1, every)
    core_stage(1)
    arrived(b_core_in, bc_s.at[0], bc_r.at[0])
    b_x_out[...] = b_core_out[...] + b_core_in[...]
    for k in range(1, NX):
        send(b_x_out, b_x_in.at[k - 1], bx_s.at[k - 1], bx_r.at[k - 1], x_dev((x + k) % NX))
    x_stage(0)
    gather_step(2, every)
    core_stage(2)
    both = b_x_out[...]
    for k in range(1, NX):
        arrived(b_x_in.at[k - 1], bx_s.at[k - 1], bx_r.at[k - 1])
        both = both + b_x_in[k - 1]
    b_y_out[...] = both
    for k in range(1, NY):
        send(b_y_out, b_y_in.at[k - 1], by_s.at[k - 1], by_r.at[k - 1], y_dev((y + k) % NY))
    x_stage(1)
    y_stage(0)
    gather_step(3, every)
    core_stage(3)
    both = b_y_out[...]
    for k in range(1, NY):
        arrived(b_y_in.at[k - 1], by_s.at[k - 1], by_r.at[k - 1])
        both = both + b_y_in[k - 1]
    inner[z] = both
    for k in range(1, NZ):
        send(inner.at[z], inner.at[z], bz_s.at[k - 1], bz_r.at[k - 1], z_dev((z + k) % NZ))
    x_stage(2)
    y_stage(1)
    gather_end(every)
    core_stage(4)
    x_stage(3)
    y_stage(2)

    for k in range(2):
        acc = jnp.zeros((HID, JOB_COLS), F32)
        for q in range(NYHI):
            blocks = [NCORE * q + c for c in range(NCORE)]
            low_at, grad_at = HLOW_AT + k * ADAPTER_RANK, GRAD_AT + k * HID
            low = held_rows(blocks, low_at, low_at + ADAPTER_RANK).astype(F32)
            wide = jnp.where(pair_mask(q), jnp.concatenate([low] * JOB_COUNT, axis=0), 0.0)
            acc = acc + mm_nt(held_rows(blocks, grad_at, grad_at + HID), wide.astype(BF16))
        gb_ref[k] = SCALE * acc
    store(3, gb_ref, gb_hbm)
    x_stage(4)
    y_stage(3)
    for k in range(1, NZ):
        arrived(inner.at[(z + NZ - k) % NZ], bz_s.at[k - 1], bz_r.at[k - 1])

    def wide_inner(k, blocks, mask):
        rows = [inner[p, k * ADAPTER_RANK:(k + 1) * ADAPTER_RANK, :] for p in blocks]
        rows = jnp.concatenate(rows, axis=1)
        wide = jnp.where(mask, jnp.concatenate([rows] * JOB_COUNT, axis=0), 0.0)
        hi = wide.astype(BF16)
        return hi, (wide - hi.astype(F32)).astype(BF16)

    for k in range(2):
        acc = jnp.zeros((FEAT, JOB_COLS), F32)
        for q in range(NYHI):
            rows = pair(0, q)
            for wide in wide_inner(k, [NCORE * q + c for c in range(NCORE)], pair_mask(q)):
                acc = acc + mm_nt(rows, wide)
        ga_ref[k] = acc
    store(2, ga_ref, ga_hbm)
    y_stage(4)
    mask = wide_mask(jobs[yhi, core])
    extra = jnp.zeros((PIECE, JOB_ROWS), F32)
    for k in range(2):
        cols = a_ref[k, pl.ds(pl.multiple_of(hid * PIECE, PIECE), PIECE), :]
        for wide in wide_inner(k, [dp], mask):
            extra = extra + mm(cols, wide)
    for c in range(NCORE):
        both = fin[c]
        for k in range(1, NY):
            arrived(y_in.at[c, k - 1], oy_s.at[0, 0], oy_r.at[c, k - 1])
            both = both + y_in[c, k - 1].astype(F32)
        fin[c] = both
    send(fin.at[1 - core], fin_in, of_s.at[0], of_r.at[0], sibling)
    arrived(fin_in, of_s.at[0], of_r.at[0])
    mixed_ref[...] = jnp.where(core == 0, fin[0], fin_in[...]).astype(BF16)
    ig_ref[...] = (jnp.where(core == 0, fin_in[...], fin[1]) + extra).astype(BF16)
    store(0, mixed_ref, mixed_hbm)
    store(1, ig_ref, ig_hbm)
    for t in range(5):
        for n, p in slots(t):
            for k, copy in y_copies(n, p):
                @pl.when(k != 0)
                def _(copy=copy):
                    copy.wait_send()
    for copy in stores:
        copy.wait()
    for copy in sent:
        copy.wait_send()


def local(tokens, token_job_index, gate_up, down, adapter_in, adapter_out, cotangent):
    hbm = pl.BlockSpec(memory_space=pltpu.HBM)
    buf = pltpu.VMEM
    tile = (PIECE, JOB_ROWS)
    ring = (2, 4, 4)
    sems = [
        (NYHI, NYLO), (NYHI, 2), (NYHI, 2), (NYHI + 1,), (NYHI - 1,), (1,),
        ring, ring, (NZ,), (NZ, NX - 1), None, (1,),
        (1,), (NX - 1,), (NY - 1,), (NZ - 1,),
    ]
    sems = [(s, s) if s else ((NZ, NYLO), (NCORE, NY - 1)) for s in sems]
    mixed, grad, grad_in, grad_out = pl.pallas_call(
        kernel,
        out_shape=[
            jax.ShapeDtypeStruct(tile, BF16),
            jax.ShapeDtypeStruct(tile, BF16),
            jax.ShapeDtypeStruct((2, FEAT, JOB_COLS), F32),
            jax.ShapeDtypeStruct((2, HID, JOB_COLS), F32),
        ],
        in_specs=[hbm] * 7,
        out_specs=[hbm] * 4,
        scratch_shapes=[
            buf((JOB_ROWS, FEAT), BF16),
            buf((1, JOB_ROWS), jnp.int32),
            buf((2, HID, FEAT), BF16),
            buf((HID, FEAT), BF16),
            buf((2, FEAT, JOB_COLS), BF16),
            buf((2, HID, JOB_COLS), BF16),
            buf(tile, BF16),
            buf(tile, BF16),
            buf((2, FEAT, JOB_COLS), F32),
            buf((2, HID, JOB_COLS), F32),
            buf((NYHI, NCORE, NYLO, NX, 2) + tile, BF16),
            buf((NYHI, NCORE, 16, JOB_ROWS), BF16),
            buf((2, FEAT, HID), BF16),
            buf((FEAT, HID), BF16),
            buf((2 * JOB_COLS, FEAT), BF16),
            buf((2, JOB_COLS, HID), BF16),
            buf((NZ, ROWS, JOB_ROWS), F32),
            buf((2, 4, ROWS, JOB_ROWS), BF16),
            buf((2, 4, ROWS, JOB_ROWS), BF16),
            buf((NZ, ROWS, JOB_ROWS), BF16),
            buf((NZ, 2, NYLO, NX) + tile, BF16),
            buf((NZ, NYLO, NX) + tile, BF16),
            buf((NZ, NYLO, NX) + tile, BF16),
            buf((NZ, NX - 1, NYLO) + tile, BF16),
            buf((NZ, NYLO) + tile, BF16),
            buf((NCORE, NY - 1) + tile, BF16),
            buf((NCORE,) + tile, F32),
            buf(tile, F32),
            buf((LOW, JOB_ROWS), F32),
            buf((LOW, JOB_ROWS), F32),
            buf((LOW, JOB_ROWS), F32),
            buf((NX - 1, LOW, JOB_ROWS), F32),
            buf((LOW, JOB_ROWS), F32),
            buf((NY - 1, LOW, JOB_ROWS), F32),
            buf((NZ, LOW, JOB_ROWS), F32),
        ] + [pltpu.SemaphoreType.DMA(s) for pair in sems for s in pair] + [
            pltpu.SemaphoreType.DMA((7,)), pltpu.SemaphoreType.DMA((4,)),
        ],
        compiler_params=pltpu.CompilerParams(
            collective_id=0, has_side_effects=True, vmem_limit_bytes=63 * 1024 * 1024
        ),
    )(
        tokens, token_job_index.reshape(1, JOB_ROWS), jnp.swapaxes(gate_up, 1, 2), down,
        adapter_in, jnp.swapaxes(adapter_out, 1, 2), cotangent.T,
    )
    return mixed.T, grad.T, grad_in, jnp.swapaxes(grad_out, 1, 2)


def solution(mesh):
    return jax.shard_map(
        local,
        mesh=mesh,
        in_specs=(
            P("dp", "width"),
            P("dp"),
            P(None, "width", ("dp", "hidden")),
            P(("dp", "hidden"), "width"),
            P(None, "width", None),
            P(None, None, ("dp", "hidden")),
            P("dp", ("width", "hidden")),
        ),
        out_specs=(
            P("dp", ("width", "hidden")),
            P("dp", ("width", "hidden")),
            P(None, "width", None),
            P(None, None, ("dp", "hidden")),
        ),
        check_vma=False,
    )
```

time: 116 us -> 89.9 us (0.78)
  the two profiles are of different devices: /device:TPU:65 before, /device:TPU:33 now
where the time goes in v2:
time: 89.9 us; the launch traced here: 89.7 us
  Pallas kernels  84 us (93%)
  local copies, waits for them, and re-layouts  5.03 us (6%)
    pallas_call x1, Pallas kernels, local(): pl.pallas_call(kernel, out_shape=[jax.ShapeDtypeStruct(tile, BF16), jax.S...  84 us
    unnamed x8, local copies, waits for them, and re-layouts  5.03 us

profile of v2, /device:TPU:33, one launch (start us, length us, event | category | flops | bytes accessed | tf_op | source)
XLA Modules:
  0.0 89.7 jit_solution(962624921014966887)
XLA Ops:
  0.6 84.0 %shard_map.102 = (bf16[64,128]{1,0:T(8,128)(2,1)}, bf16[64,128]{1,0:T(8,128)(2,1)}, f32[2,512,256]{2,1,0:T(8,128)}, f32[2,224,256]{2,1,0:T(8,128)}) custom-call(bf16[128,512]{1,0:T(8,128)(2,1)} %tok_hbm.1, s32[1,128]{1,0:T(1,128)} %bitcast.13, bf16[2,224,512]{2,1,0:T(8,128)(2,1)} %bitcast.8, bf16[224,512]{1,0:T(8,128)(2,1)} %dn_hbm.1, ...), custom_call_target="tpu_custom_call" | custom-call | tf_op jit(solution)/shard_map/pallas_call | solution.py:471
  84.7 0.0 copy-start.1
  84.7 1.3 %copy.15 = bf16[128,64]{0,1:T(8,128)(2,1)} copy(bf16[128,64]{0,1:T(8,128)(2,1)} %bitcast.12) | data formatting | bytes 32768
  86.0 0.0 copy-done.1
  86.0 0.6 copy.16
  86.6 0.0 copy-start
  86.6 2.3 %copy.17 = f32[2,512,256]{2,1,0:T(8,128)} copy(f32[2,512,256]{2,1,0:T(8,128)} %get-tuple-element.18) | data formatting | bytes 2097152
  88.9 0.0 copy-done
  88.9 0.8 copy.18
Async XLA Ops:
  84.7 1.3 %copy-start.1 = (bf16[64,128]{1,0:T(8,128)(2,1)S(1)}, bf16[64,128]{1,0:T(8,128)(2,1)}, u32[]{:S(2)}) copy-start(bf16[64,128]{1,0:T(8,128)(2,1)} %get-tuple-element.9) | copy-start | bytes 49156
  86.6 2.3 %copy-start = (f32[2,224,256]{2,1,0:T(8,128)S(1)}, f32[2,224,256]{2,1,0:T(8,128)}, u32[]{:S(2)}) copy-start(f32[2,224,256]{2,1,0:T(8,128)} %get-tuple-element.11) | copy-start | bytes 1376260

commit v3 on v2

--- a/solution.py
+++ b/solution.py
@@ -41,10 +41,10 @@
     mixed_ref, ig_ref, ga_ref, gb_ref,
     xc, jobs, gu, dnt, at, bn,
     part, ring_out, ring_in, held,
-    outp, core_in, x_out, x_in, y_out, y_in, fin, fin_in,
+    outp, core_in, x_out, x_in, y_out, y_in, fin,
     b_core_out, b_core_in, b_x_out, b_x_in, b_y_out, b_y_in, inner,
     ty_s, ty_r, tx_s, tx_r, tf_s, tf_r, tc_s, tc_r, jy_s, jy_r, jc_s, jc_r,
-    rs_s, rs_r, zg_s, zg_r, oc_s, oc_r, ox_s, ox_r, oy_s, oy_r, of_s, of_r,
+    rs_s, rs_r, zg_s, zg_r, oc_s, oc_r, ox_s, ox_r, oy_s, oy_r,
     bc_s, bc_r, bx_s, bx_r, by_s, by_r, bz_s, bz_r, load_s, store_s,
 ):
     dp = lax.axis_index("dp")
@@ -59,6 +59,9 @@
     def y_dev(other):
         return ((other // NYLO) * NCORE + core, z, (other % NYLO) * NX + x)
 
+    def final_dev(other, other_core):
+        return ((other // NYLO) * NCORE + other_core, z, (other % NYLO) * NX + x)
+
     def x_dev(other):
         return (dp, z, ylo * NX + other)
 
@@ -100,6 +103,7 @@
     barrier = pltpu.get_barrier_semaphore()
     partners = [sibling]
     partners += [y_dev((y + k) % NY) for k in range(1, NY)]
+    partners += [final_dev((y + k) % NY, 1 - core) for k in range(1, NY)]
     partners += [x_dev((x + k) % NX) for k in range(1, NX)]
     partners += [z_dev((z + k) % NZ) for k in range(1, NZ)]
     for dev in partners:
@@ -218,7 +222,7 @@
         ready = []
         for way in range(2):
             cuts = [c for c in chunks if t > 0 or c % 2 == way]
-            cuts.sort(key=lambda c: c % 2 == way)
+            cuts.sort(key=lambda c: (c // 2 if t > 1 else 0, c % 2 == way))
             ready.append(cuts)
         for cuts in zip(*ready):
             for way, c in enumerate(cuts):
@@ -297,11 +301,11 @@
         for low in range(NYLO):
             other = (p // NCORE) * NYLO + low
             k = (other + NY - y) % NY
-            slot = (k + NY - 1) % NY
-            yield k, pltpu.make_async_remote_copy(
-                src_ref=y_out.at[n, low], dst_ref=y_in.at[p % NCORE, slot],
-                send_sem=oy_s.at[n, low], recv_sem=oy_r.at[p % NCORE, slot],
-                device_id=y_dev(other), device_id_type=pl.DeviceIdType.MESH,
+            here = (p == dp) & (low == ylo)
+            yield low, here, pltpu.make_async_remote_copy(
+                src_ref=y_out.at[n, low], dst_ref=y_in.at[core, k],
+                send_sem=oy_s.at[n, low], recv_sem=oy_r.at[core, k],
+                device_id=final_dev(other, p % NCORE), device_id_type=pl.DeviceIdType.MESH,
             )
 
     def y_stage(t):
@@ -311,14 +315,14 @@
                 arrived(x_in.at[n, k - 1], ox_s.at[n, k - 1], ox_r.at[n, k - 1])
                 both = both + x_in[n, k - 1].astype(F32)
             y_out[n] = both.astype(BF16)
-            for k, copy in y_copies(n, p):
-                @pl.when(k != 0)
+            for low, here, copy in y_copies(n, p):
+                @pl.when(jnp.logical_not(here))
                 def _(copy=copy):
                     copy.start()
 
-            @pl.when(p // NCORE == yhi)
-            def _(n=n, p=p):
-                fin[p % NCORE] = y_out[n, ylo].astype(F32)
+                @pl.when(here)
+                def _(n=n, low=low):
+                    fin[...] = y_out[n, low].astype(F32)
 
     forward, backward = (0, 1), (2, 3)
     every = forward + backward
@@ -396,6 +400,7 @@
     x_stage(3)
     y_stage(2)
 
+    x_stage(4)
     for k in range(2):
         acc = jnp.zeros((HID, JOB_COLS), F32)
         for q in range(NYHI):
@@ -406,7 +411,6 @@
             acc = acc + mm_nt(held_rows(blocks, grad_at, grad_at + HID), wide.astype(BF16))
         gb_ref[k] = SCALE * acc
     store(3, gb_ref, gb_hbm)
-    x_stage(4)
     y_stage(3)
     for k in range(1, NZ):
         arrived(inner.at[(z + NZ - k) % NZ], bz_s.at[k - 1], bz_r.at[k - 1])
@@ -433,28 +437,43 @@
         cols = a_ref[k, pl.ds(pl.multiple_of(hid * PIECE, PIECE), PIECE), :]
         for wide in wide_inner(k, [dp], mask):
             extra = extra + mm(cols, wide)
+    sums = []
     for c in range(NCORE):
-        both = fin[c]
+        both = jnp.zeros((PIECE, JOB_ROWS), F32)
         for k in range(1, NY):
-            arrived(y_in.at[c, k - 1], oy_s.at[0, 0], oy_r.at[c, k - 1])
-            both = both + y_in[c, k - 1].astype(F32)
-        fin[c] = both
-    send(fin.at[1 - core], fin_in, of_s.at[0], of_r.at[0], sibling)
-    arrived(fin_in, of_s.at[0], of_r.at[0])
-    mixed_ref[...] = jnp.where(core == 0, fin[0], fin_in[...]).astype(BF16)
-    ig_ref[...] = (jnp.where(core == 0, fin_in[...], fin[1]) + extra).astype(BF16)
+            arrived(y_in.at[c, k], oy_s.at[0, 0], oy_r.at[c, k])
+            both = both + y_in[c, k].astype(F32)
+        sums.append(both)
+    arrived(y_in.at[1 - core, 0], oy_s.at[0, 0], oy_r.at[1 - core, 0])
+    near = y_in[1 - core, 0].astype(F32)
+    mixed_ref[...] = (sums[0] + jnp.where(core == 0, fin[...], near)).astype(BF16)
+    ig_ref[...] = (sums[1] + extra + jnp.where(core == 0, near, fin[...])).astype(BF16)
     store(0, mixed_ref, mixed_hbm)
     store(1, ig_ref, ig_hbm)
     for t in range(5):
         for n, p in slots(t):
-            for k, copy in y_copies(n, p):
-                @pl.when(k != 0)
+            for _, here, copy in y_copies(n, p):
+                @pl.when(jnp.logical_not(here))
                 def _(copy=copy):
                     copy.wait_send()
     for copy in stores:
         copy.wait()
     for copy in sent:
         copy.wait_send()
+
+
+def hand_over(*refs):
+    srcs, dsts, held = refs[0:4], refs[4:8], refs[8:12]
+    load_sem, store_sem = refs[12:14]
+    loads = [pltpu.make_async_copy(srcs[i], held[i], load_sem.at[i]) for i in range(4)]
+    stores = [pltpu.make_async_copy(held[i], dsts[i], store_sem.at[i]) for i in range(4)]
+    for copy in loads:
+        copy.start()
+    for load, copy in zip(loads, stores):
+        load.wait()
+        copy.start()
+    for copy in stores:
+        copy.wait()
 
 
 def local(tokens, token_job_index, gate_up, down, adapter_in, adapter_out, cotangent):
@@ -464,11 +483,11 @@
     ring = (2, 4, 4)
     sems = [
         (NYHI, NYLO), (NYHI, 2), (NYHI, 2), (NYHI + 1,), (NYHI - 1,), (1,),
-        ring, ring, (NZ,), (NZ, NX - 1), None, (1,),
+        ring, ring, (NZ,), (NZ, NX - 1), None,
         (1,), (NX - 1,), (NY - 1,), (NZ - 1,),
     ]
-    sems = [(s, s) if s else ((NZ, NYLO), (NCORE, NY - 1)) for s in sems]
-    mixed, grad, grad_in, grad_out = pl.pallas_call(
+    sems = [(s, s) if s else ((NZ, NYLO), (NCORE, NY)) for s in sems]
+    outs = pl.pallas_call(
         kernel,
         out_shape=[
             jax.ShapeDtypeStruct(tile, BF16),
@@ -504,8 +523,7 @@
             buf((NZ, NYLO, NX) + tile, BF16),
             buf((NZ, NX - 1, NYLO) + tile, BF16),
             buf((NZ, NYLO) + tile, BF16),
-            buf((NCORE, NY - 1) + tile, BF16),
-            buf((NCORE,) + tile, F32),
+            buf((NCORE, NY) + tile, BF16),
             buf(tile, F32),
             buf((LOW, JOB_ROWS), F32),
             buf((LOW, JOB_ROWS), F32),
@@ -524,6 +542,15 @@
         tokens, token_job_index.reshape(1, JOB_ROWS), jnp.swapaxes(gate_up, 1, 2), down,
         adapter_in, jnp.swapaxes(adapter_out, 1, 2), cotangent.T,
     )
+    dma = pltpu.SemaphoreType.DMA((4,))
+    mixed, grad, grad_in, grad_out = pl.pallas_call(
+        hand_over,
+        out_shape=[jax.ShapeDtypeStruct(out.shape, out.dtype) for out in outs],
+        in_specs=[hbm] * 4,
+        out_specs=[hbm] * 4,
+        scratch_shapes=[buf(out.shape, out.dtype) for out in outs] + [dma, dma],
+        compiler_params=pltpu.CompilerParams(vmem_limit_bytes=63 * 1024 * 1024),
+    )(*outs)
     return mixed.T, grad.T, grad_in, jnp.swapaxes(grad_out, 1, 2)
 
 

time: 89.9 us -> 85.6 us (0.952)
  the two profiles are of different devices: /device:TPU:33 before, /device:TPU:40 now
where the time goes in v3:
time: 85.6 us; the launch traced here: 85.4 us
  Pallas kernels  84.7 us (99%)
    pallas_call x1, Pallas kernels, local(): pl.pallas_call(kernel, out_shape=[jax.ShapeDtypeStruct(tile, BF16), jax.S...  82.3 us
    pallas_call x1, Pallas kernels, local(): pl.pallas_call(hand_over, out_shape=[jax.ShapeDtypeStruct(out.shape, out....  2.44 us

profile of v3, /device:TPU:40, one launch (start us, length us, event | category | flops | bytes accessed | tf_op | source)
XLA Modules:
  0.0 85.4 jit_solution(17870699143206876849)
XLA Ops:
  0.6 82.3 %shard_map.102 = (bf16[64,128]{1,0:T(8,128)(2,1)}, bf16[64,128]{1,0:T(8,128)(2,1)}, f32[2,512,256]{2,1,0:T(8,128)}, f32[2,224,256]{2,1,0:T(8,128)}) custom-call(bf16[128,512]{1,0:T(8,128)(2,1)} %tok_hbm.1, s32[1,128]{1,0:T(1,128)} %bitcast.10, bf16[2,224,512]{2,1,0:T(8,128)(2,1)} %bitcast.7, bf16[224,512]{1,0:T(8,128)(2,1)} %dn_hbm.1, ...), custom_call_target="tpu_custom_call" | custom-call | tf_op jit(solution)/shard_map/pallas_call | solution.py:490
  82.9 2.4 %shard_map.103 = (bf16[64,128]{1,0:T(8,128)(2,1)}, bf16[64,128]{1,0:T(8,128)(2,1)}, f32[2,512,256]{2,1,0:T(8,128)}, f32[2,224,256]{2,1,0:T(8,128)}) custom-call(bf16[64,128]{1,0:T(8,128)(2,1)} %get-tuple-element.12.refs_0_, bf16[64,128]{1,0:T(8,128)(2,1)} %get-tuple-element.13.refs_1_, f32[2,512,256]{2,1,0:T(8,128)} %get-tuple-element.14.refs_2_, ...), custom_call_target="tpu_custom_call" | custom-call | tf_op jit(solution)/shard_map/pallas_call | solution.py:546

commit v4 on v3

--- a/solution.py
+++ b/solution.py
@@ -366,15 +366,13 @@
         ).sum(0)
     send(b_core_out, b_core_in, bc_s.at[0], bc_r.at[0], sibling)
     core_stage(0)
-    gather_step(1, every)
-    core_stage(1)
     arrived(b_core_in, bc_s.at[0], bc_r.at[0])
     b_x_out[...] = b_core_out[...] + b_core_in[...]
     for k in range(1, NX):
         send(b_x_out, b_x_in.at[k - 1], bx_s.at[k - 1], bx_r.at[k - 1], x_dev((x + k) % NX))
+    gather_step(1, every)
+    core_stage(1)
     x_stage(0)
-    gather_step(2, every)
-    core_stage(2)
     both = b_x_out[...]
     for k in range(1, NX):
         arrived(b_x_in.at[k - 1], bx_s.at[k - 1], bx_r.at[k - 1])
@@ -382,10 +380,13 @@
     b_y_out[...] = both
     for k in range(1, NY):
         send(b_y_out, b_y_in.at[k - 1], by_s.at[k - 1], by_r.at[k - 1], y_dev((y + k) % NY))
+    gather_step(2, every)
+    core_stage(2)
     x_stage(1)
     y_stage(0)
     gather_step(3, every)
     core_stage(3)
+    x_stage(2)
     both = b_y_out[...]
     for k in range(1, NY):
         arrived(b_y_in.at[k - 1], by_s.at[k - 1], by_r.at[k - 1])
@@ -393,14 +394,12 @@
     inner[z] = both
     for k in range(1, NZ):
         send(inner.at[z], inner.at[z], bz_s.at[k - 1], bz_r.at[k - 1], z_dev((z + k) % NZ))
-    x_stage(2)
     y_stage(1)
     gather_end(every)
     core_stage(4)
     x_stage(3)
+    x_stage(4)
     y_stage(2)
-
-    x_stage(4)
     for k in range(2):
         acc = jnp.zeros((HID, JOB_COLS), F32)
         for q in range(NYHI):
@@ -412,6 +411,7 @@
         gb_ref[k] = SCALE * acc
     store(3, gb_ref, gb_hbm)
     y_stage(3)
+    y_stage(4)
     for k in range(1, NZ):
         arrived(inner.at[(z + NZ - k) % NZ], bz_s.at[k - 1], bz_r.at[k - 1])
 
@@ -430,7 +430,6 @@
                 acc = acc + mm_nt(rows, wide)
         ga_ref[k] = acc
     store(2, ga_ref, ga_hbm)
-    y_stage(4)
     mask = wide_mask(jobs[yhi, core])
     extra = jnp.zeros((PIECE, JOB_ROWS), F32)
     for k in range(2):
@@ -465,10 +464,16 @@
 def hand_over(*refs):
     srcs, dsts, held = refs[0:4], refs[4:8], refs[8:12]
     load_sem, store_sem = refs[12:14]
-    loads = [pltpu.make_async_copy(srcs[i], held[i], load_sem.at[i]) for i in range(4)]
-    stores = [pltpu.make_async_copy(held[i], dsts[i], store_sem.at[i]) for i in range(4)]
-    for copy in loads:
-        copy.start()
+    cuts = [(i, ()) for i in range(2)] + [
+        (i, (k, pl.ds(j * rows, rows))) for i, rows in ((2, 256), (3, 112))
+        for k in range(2) for j in range(2)
+    ]
+    loads, stores = [], []
+    for n, (i, cut) in enumerate(cuts):
+        src, own, dst = (ref.at[cut] if cut else ref for ref in (srcs[i], held[i], dsts[i]))
+        loads.append(pltpu.make_async_copy(src, own, load_sem.at[n]))
+        stores.append(pltpu.make_async_copy(own, dst, store_sem.at[n]))
+        loads[-1].start()
     for load, copy in zip(loads, stores):
         load.wait()
         copy.start()
@@ -542,7 +547,7 @@
         tokens, token_job_index.reshape(1, JOB_ROWS), jnp.swapaxes(gate_up, 1, 2), down,
         adapter_in, jnp.swapaxes(adapter_out, 1, 2), cotangent.T,
     )
-    dma = pltpu.SemaphoreType.DMA((4,))
+    dma = pltpu.SemaphoreType.DMA((10,))
     mixed, grad, grad_in, grad_out = pl.pallas_call(
         hand_over,
         out_shape=[jax.ShapeDtypeStruct(out.shape, out.dtype) for out in outs],

time: 85.6 us -> 83.2 us (0.972)
  Pallas kernels: 84.7 us -> 82.3 us
    pallas_call x1, Pallas kernels: 82.3 us -> 80 us  [local(): pl.pallas_call(kernel, out_shape=[jax.ShapeDtypeStruct(tile, BF16), jax.S...]
where the time goes in v4:
time: 83.2 us; the launch traced here: 83 us
  Pallas kernels  82.3 us (99%)
    pallas_call x1, Pallas kernels, local(): pl.pallas_call(kernel, out_shape=[jax.ShapeDtypeStruct(tile, BF16), jax.S...  80 us
    pallas_call x1, Pallas kernels, local(): pl.pallas_call(hand_over, out_shape=[jax.ShapeDtypeStruct(out.shape, out....  2.26 us

profile of v4, /device:TPU:40, one launch (start us, length us, event | category | flops | bytes accessed | tf_op | source)
XLA Modules:
  0.0 83.0 jit_solution(5544489989602044038)
XLA Ops:
  0.6 80.0 %shard_map.102 = (bf16[64,128]{1,0:T(8,128)(2,1)}, bf16[64,128]{1,0:T(8,128)(2,1)}, f32[2,512,256]{2,1,0:T(8,128)}, f32[2,224,256]{2,1,0:T(8,128)}) custom-call(bf16[128,512]{1,0:T(8,128)(2,1)} %tok_hbm.1, s32[1,128]{1,0:T(1,128)} %bitcast.10, bf16[2,224,512]{2,1,0:T(8,128)(2,1)} %bitcast.7, bf16[224,512]{1,0:T(8,128)(2,1)} %dn_hbm.1, ...), custom_call_target="tpu_custom_call" | custom-call | tf_op jit(solution)/shard_map/pallas_call | solution.py:495
  80.7 2.3 %shard_map.103 = (bf16[64,128]{1,0:T(8,128)(2,1)}, bf16[64,128]{1,0:T(8,128)(2,1)}, f32[2,512,256]{2,1,0:T(8,128)}, f32[2,224,256]{2,1,0:T(8,128)}) custom-call(bf16[64,128]{1,0:T(8,128)(2,1)} %get-tuple-element.12.refs_0_, bf16[64,128]{1,0:T(8,128)(2,1)} %get-tuple-element.13.refs_1_, f32[2,512,256]{2,1,0:T(8,128)} %get-tuple-element.14.refs_2_, ...), custom_call_target="tpu_custom_call" | custom-call | tf_op jit(solution)/shard_map/pallas_call | solution.py:551

commit v5 on v4

--- a/solution.py
+++ b/solution.py
@@ -85,6 +85,14 @@
             device_id=sibling, device_id_type=pl.DeviceIdType.MESH,
         ).wait_recv()
 
+    barrier = pltpu.get_barrier_semaphore()
+    far_first = (4, 3, 5, 2, 6, 1, 7)
+    partners = [z_dev((z + k) % NZ) for k in far_first]
+    for k in far_first:
+        partners += [y_dev((y + k) % NY), final_dev((y + k) % NY, 1 - core)]
+    partners += [x_dev((x + k) % NX) for k in (2, 1, 3)] + [sibling]
+    for dev in partners:
+        pl.semaphore_signal(barrier, inc=1, device_id=dev, device_id_type=pl.DeviceIdType.MESH)
     own_cot = xc.at[yhi, core, ylo, x, 1]
     loads = {}
     for i, (src, dst) in enumerate((
@@ -100,14 +108,6 @@
         copy.start()
         stores.append(copy)
 
-    barrier = pltpu.get_barrier_semaphore()
-    partners = [sibling]
-    partners += [y_dev((y + k) % NY) for k in range(1, NY)]
-    partners += [final_dev((y + k) % NY, 1 - core) for k in range(1, NY)]
-    partners += [x_dev((x + k) % NX) for k in range(1, NX)]
-    partners += [z_dev((z + k) % NZ) for k in range(1, NZ)]
-    for dev in partners:
-        pl.semaphore_signal(barrier, inc=1, device_id=dev, device_id_type=pl.DeviceIdType.MESH)
     eye = (
         lax.broadcasted_iota(jnp.int32, (256, 256), 0)
         == lax.broadcasted_iota(jnp.int32, (256, 256), 1)
@@ -324,6 +324,13 @@
                 def _(n=n, low=low):
                     fin[...] = y_out[n, low].astype(F32)
 
+    def y_settle(t):
+        for n, p in slots(t):
+            for _, here, copy in y_copies(n, p):
+                @pl.when(jnp.logical_not(here))
+                def _(copy=copy):
+                    copy.wait_send()
+
     forward, backward = (0, 1), (2, 3)
     every = forward + backward
     forward_sums(far // NCORE)
@@ -373,6 +380,7 @@
     gather_step(1, every)
     core_stage(1)
     x_stage(0)
+    x_stage(1)
     both = b_x_out[...]
     for k in range(1, NX):
         arrived(b_x_in.at[k - 1], bx_s.at[k - 1], bx_r.at[k - 1])
@@ -382,11 +390,12 @@
         send(b_y_out, b_y_in.at[k - 1], by_s.at[k - 1], by_r.at[k - 1], y_dev((y + k) % NY))
     gather_step(2, every)
     core_stage(2)
-    x_stage(1)
     y_stage(0)
+    x_stage(2)
     gather_step(3, every)
     core_stage(3)
-    x_stage(2)
+    y_stage(1)
+    x_stage(3)
     both = b_y_out[...]
     for k in range(1, NY):
         arrived(b_y_in.at[k - 1], by_s.at[k - 1], by_r.at[k - 1])
@@ -394,12 +403,10 @@
     inner[z] = both
     for k in range(1, NZ):
         send(inner.at[z], inner.at[z], bz_s.at[k - 1], bz_r.at[k - 1], z_dev((z + k) % NZ))
-    y_stage(1)
     gather_end(every)
     core_stage(4)
-    x_stage(3)
+    y_stage(2)
     x_stage(4)
-    y_stage(2)
     for k in range(2):
         acc = jnp.zeros((HID, JOB_COLS), F32)
         for q in range(NYHI):
@@ -436,6 +443,10 @@
         cols = a_ref[k, pl.ds(pl.multiple_of(hid * PIECE, PIECE), PIECE), :]
         for wide in wide_inner(k, [dp], mask):
             extra = extra + mm(cols, wide)
+    for copy in sent:
+        copy.wait_send()
+    for t in range(4):
+        y_settle(t)
     sums = []
     for c in range(NCORE):
         both = jnp.zeros((PIECE, JOB_ROWS), F32)
@@ -449,16 +460,9 @@
     ig_ref[...] = (sums[1] + extra + jnp.where(core == 0, near, fin[...])).astype(BF16)
     store(0, mixed_ref, mixed_hbm)
     store(1, ig_ref, ig_hbm)
-    for t in range(5):
-        for n, p in slots(t):
-            for _, here, copy in y_copies(n, p):
-                @pl.when(jnp.logical_not(here))
-                def _(copy=copy):
-                    copy.wait_send()
+    y_settle(4)
     for copy in stores:
         copy.wait()
-    for copy in sent:
-        copy.wait_send()
 
 
 def hand_over(*refs):

time: 83.2 us -> 81.3 us (0.977)
  Pallas kernels: 82.3 us -> 80.5 us
    pallas_call x1, Pallas kernels: 80 us -> 78.2 us  [local(): pl.pallas_call(kernel, out_shape=[jax.ShapeDtypeStruct(tile, BF16), jax.S...]
where the time goes in v5:
time: 81.3 us; the launch traced here: 81.1 us
  Pallas kernels  80.5 us (99%)
    pallas_call x1, Pallas kernels, local(): pl.pallas_call(kernel, out_shape=[jax.ShapeDtypeStruct(tile, BF16), jax.S...  78.2 us
    pallas_call x1, Pallas kernels, local(): pl.pallas_call(hand_over, out_shape=[jax.ShapeDtypeStruct(out.shape, out....  2.26 us

profile of v5, /device:TPU:40, one launch (start us, length us, event | category | flops | bytes accessed | tf_op | source)
XLA Modules:
  0.0 81.1 jit_solution(2136443697368149586)
XLA Ops:
  0.6 78.2 %shard_map.102 = (bf16[64,128]{1,0:T(8,128)(2,1)}, bf16[64,128]{1,0:T(8,128)(2,1)}, f32[2,512,256]{2,1,0:T(8,128)}, f32[2,224,256]{2,1,0:T(8,128)}) custom-call(bf16[128,512]{1,0:T(8,128)(2,1)} %tok_hbm.1, s32[1,128]{1,0:T(1,128)} %bitcast.10, bf16[2,224,512]{2,1,0:T(8,128)(2,1)} %bitcast.7, bf16[224,512]{1,0:T(8,128)(2,1)} %dn_hbm.1, ...), custom_call_target="tpu_custom_call" | custom-call | tf_op jit(solution)/shard_map/pallas_call | solution.py:499
  78.8 2.3 %shard_map.103 = (bf16[64,128]{1,0:T(8,128)(2,1)}, bf16[64,128]{1,0:T(8,128)(2,1)}, f32[2,512,256]{2,1,0:T(8,128)}, f32[2,224,256]{2,1,0:T(8,128)}) custom-call(bf16[64,128]{1,0:T(8,128)(2,1)} %get-tuple-element.12.refs_0_, bf16[64,128]{1,0:T(8,128)(2,1)} %get-tuple-element.13.refs_1_, f32[2,512,256]{2,1,0:T(8,128)} %get-tuple-element.14.refs_2_, ...), custom_call_target="tpu_custom_call" | custom-call | tf_op jit(solution)/shard_map/pallas_call | solution.py:555

commit v6 on v5

--- a/solution.py
+++ b/solution.py
@@ -377,9 +377,9 @@
     b_x_out[...] = b_core_out[...] + b_core_in[...]
     for k in range(1, NX):
         send(b_x_out, b_x_in.at[k - 1], bx_s.at[k - 1], bx_r.at[k - 1], x_dev((x + k) % NX))
+    x_stage(0)
     gather_step(1, every)
     core_stage(1)
-    x_stage(0)
     x_stage(1)
     both = b_x_out[...]
     for k in range(1, NX):

time: 81.3 us -> 81.3 us (level)
  no operation moved by 1% of the time
where the time goes in v6:
time: 81.3 us; the launch traced here: 81 us
  Pallas kernels  80.4 us (99%)
    pallas_call x1, Pallas kernels, local(): pl.pallas_call(kernel, out_shape=[jax.ShapeDtypeStruct(tile, BF16), jax.S...  78.1 us
    pallas_call x1, Pallas kernels, local(): pl.pallas_call(hand_over, out_shape=[jax.ShapeDtypeStruct(out.shape, out....  2.26 us

profile of v6, /device:TPU:40, one launch (start us, length us, event | category | flops | bytes accessed | tf_op | source)
XLA Modules:
  0.0 81.0 jit_solution(6501857903151902131)
XLA Ops:
  0.6 78.1 %shard_map.102 = (bf16[64,128]{1,0:T(8,128)(2,1)}, bf16[64,128]{1,0:T(8,128)(2,1)}, f32[2,512,256]{2,1,0:T(8,128)}, f32[2,224,256]{2,1,0:T(8,128)}) custom-call(bf16[128,512]{1,0:T(8,128)(2,1)} %tok_hbm.1, s32[1,128]{1,0:T(1,128)} %bitcast.10, bf16[2,224,512]{2,1,0:T(8,128)(2,1)} %bitcast.7, bf16[224,512]{1,0:T(8,128)(2,1)} %dn_hbm.1, ...), custom_call_target="tpu_custom_call" | custom-call | tf_op jit(solution)/shard_map/pallas_call | solution.py:499
  78.8 2.3 %shard_map.103 = (bf16[64,128]{1,0:T(8,128)(2,1)}, bf16[64,128]{1,0:T(8,128)(2,1)}, f32[2,512,256]{2,1,0:T(8,128)}, f32[2,224,256]{2,1,0:T(8,128)}) custom-call(bf16[64,128]{1,0:T(8,128)(2,1)} %get-tuple-element.12.refs_0_, bf16[64,128]{1,0:T(8,128)(2,1)} %get-tuple-element.13.refs_1_, f32[2,512,256]{2,1,0:T(8,128)} %get-tuple-element.14.refs_2_, ...), custom_call_target="tpu_custom_call" | custom-call | tf_op jit(solution)/shard_map/pallas_call | solution.py:555
